TPU v7x, 32 devices: a whole 2x2x4 slice. The times are simulated.
32 devices in a mesh: groups: 2 (over y), row: 4 (over x, core), col: 4 (over z).
Axes of the slice: x: 2, y: 2, z: 4, core: 2. Of those that a mesh axis runs over, the one named last changes fastest.
Arguments:
- tokens: bfloat16 [1024, 4096], P(('groups', 'col'), 'row'), parts along dimension 0, may hold values from -6 to 6
- cotangent: bfloat16 [1024, 4096], P(('groups', 'col'), 'row'), parts along dimension 0, may hold values from -3 to 3
- gate_weight: bfloat16 [4096, 16384], P('row', 'col'), may hold values from -0.125 to 0.125
- up_weight: bfloat16 [4096, 16384], P('row', 'col'), may hold values from -0.125 to 0.125
- down_weight: bfloat16 [16384, 4096], P('col', 'row'), may hold values from -0.0625 to 0.0625
- gate_keep: int32 [32, 128], P('row', 'col'), may hold values from 0 to 1, as said below
- down_keep: int32 [128, 32], P('col', 'row'), may hold values from 0 to 1, as said below
Outputs:
- token_gradient: bfloat16 [1024, 4096], P(('groups', 'col'), 'row'), parts along dimension 0
- gate_gradient: bfloat16 [8192, 16384], P(('groups', 'row'), 'col'), parts along dimension 0
- up_gradient: bfloat16 [8192, 16384], P(('groups', 'row'), 'col'), parts along dimension 0
- down_gradient: bfloat16 [32768, 4096], P(('groups', 'col'), 'row'), parts along dimension 0
There are 2 independent parts, one for each index of `groups`. A program takes and returns all parts, laid end to end along the dimension named above; an argument that names none is the same for every part. Nothing has to cross between parts.
Inputs may be any that keep to these rules, and one draw needn't show every extreme that they name: `gate_keep`: exactly half of the entries are 1 (block kept), the others 0. `down_keep`: exactly half of the entries are 1 (block kept), the others 0.
All inputs are finite; a program needn't handle non-finite values.
Results may differ from a plain program's by a relative error of at most 0.019.
Values may be sent and summed in bfloat16 or wider, within the bound.
A program may use at most 192 MiB of HBM per device.

v0:
```python
import jax
import jax.numpy as jnp
from jax import lax
from jax.sharding import PartitionSpec as P

BLK = 128


CONTRACT_ROWS = (((0,), (0,)), ((), ()))
CONTRACT_COLUMNS = (((1,), (1,)), ((), ()))


def expand_mask(keep):
    return jnp.repeat(jnp.repeat(keep, BLK, axis=0), BLK, axis=1).astype(jnp.bfloat16)


def dense_ahead(left, weight):
    return jnp.dot(left, weight, preferred_element_type=jnp.float32)


def dense_behind(left, weight):
    return lax.dot_general(left, weight, CONTRACT_COLUMNS, preferred_element_type=jnp.float32)


def dense_outer(left, right, keep):
    product = lax.dot_general(left, right, CONTRACT_ROWS, preferred_element_type=jnp.float32)
    return product * expand_mask(keep).astype(jnp.float32)


def gate_up_deltas(hidden_delta, gate, up):
    sigma = jax.nn.sigmoid(gate)
    gate_delta = hidden_delta * up * sigma * (1.0 + gate * (1.0 - sigma))
    up_delta = hidden_delta * gate * sigma
    return (gate_delta.astype(jnp.bfloat16), up_delta.astype(jnp.bfloat16))


def on_device(tokens, cotangent, gate_weight, up_weight, down_weight, gate_keep, down_keep):
    token_rows, cotangent_rows = (
        lax.all_gather(tokens, "col", axis=0, tiled=True),
        lax.all_gather(cotangent, "col", axis=0, tiled=True),
    )
    width = gate_weight.shape[1]
    gate_mask = expand_mask(gate_keep)
    down_mask = expand_mask(down_keep)
    gate_kept = gate_weight * gate_mask
    up_kept = up_weight * gate_mask
    down_kept = down_weight * down_mask
    joined = lax.psum_scatter(
        jnp.concatenate(
            [
                jnp.concatenate(
                    [dense_ahead(token_rows, gate_kept), dense_ahead(token_rows, up_kept)], axis=1
                ),
                dense_behind(cotangent_rows, down_kept),
            ],
            axis=1,
        ).astype(jnp.bfloat16),
        "row",
        scatter_dimension=0,
        tiled=True,
    ).astype(jnp.float32)
    gate = joined[:, :width]
    up = joined[:, width : 2 * width]
    hidden_delta = joined[:, 2 * width :]
    hidden = (jax.nn.silu(gate) * up).astype(jnp.bfloat16)
    gate_delta, up_delta = gate_up_deltas(hidden_delta, gate, up)
    hidden_all, gate_all, up_all = (
        lax.all_gather(hidden, "row", axis=0, tiled=True),
        lax.all_gather(gate_delta, "row", axis=0, tiled=True),
        lax.all_gather(up_delta, "row", axis=0, tiled=True),
    )
    down_gradient = dense_outer(hidden_all, cotangent_rows, down_keep).astype(jnp.bfloat16)
    gate_gradient = dense_outer(token_rows, gate_all, gate_keep).astype(jnp.bfloat16)
    up_gradient = dense_outer(token_rows, up_all, gate_keep).astype(jnp.bfloat16)
    token_gradient = lax.psum_scatter(
        (dense_behind(gate_all, gate_kept) + dense_behind(up_all, up_kept)).astype(jnp.bfloat16),
        "col",
        scatter_dimension=0,
        tiled=True,
    )
    return (token_gradient, gate_gradient, up_gradient, down_gradient)


def solution(mesh):
    placed = (
        P(("groups", "col"), "row"),
        P(("groups", "col"), "row"),
        P("row", "col"),
        P("row", "col"),
        P("col", "row"),
        P("row", "col"),
        P("col", "row"),
    )
    return jax.shard_map(
        on_device,
        mesh=mesh,
        in_specs=placed,
        out_specs=(
            P(("groups", "col"), "row"),
            P(("groups", "row"), "col"),
            P(("groups", "row"), "col"),
            P(("groups", "col"), "row"),
        ),
        check_vma=False,
    )
```

profile of v0, /device:TPU:0, one launch (start us, length us, event | category | flops | bytes accessed | tf_op | source)
XLA Modules:
  0.0 383.0 jit_solution(11299957182974376428)
XLA Ops:
  7.9 0.7 all-gather.8.cloned.1.call-update
  10.4 12.0 %copy.18 = bf16[1024,4096]{0,1:T(8,128)(2,1)} copy(bf16[1024,4096]{1,0:T(8,128)(2,1)} %param.9) | data formatting | bytes 16777216 | tf_op args[2]
  22.4 11.9 %copy.19 = bf16[1024,4096]{0,1:T(8,128)(2,1)} copy(bf16[1024,4096]{1,0:T(8,128)(2,1)} %param.10) | data formatting | bytes 16777216 | tf_op args[3]
  34.3 11.5 %bitcast_multiply_fusion.1 = (bf16[1024,4096]{0,1:T(8,128)(2,1)}, bf16[1024,4096]{0,1:T(8,128)(2,1)}) fusion(bf16[1024,4096]{0,1:T(8,128)(2,1)} %copy.18, bf16[1024,32]{0,1:T(8,128)(2,1)S(1)} %bitcast.54, bf16[1024,4096]{0,1:T(8,128)(2,1)} %copy.19), kind=kLoop, calls=%fused_computation.3 | loop fusion | flops 8388608 | bytes 33619968 | tf_op jit(solution)/shard_map/mul | solution.py:45
  45.8 10.5 %fusion.6 = bf16[512,4096]{0,1:T(8,128)(2,1)} fusion(bf16[1024,4096]{0,1:T(8,128)(2,1)} %get-tuple-element.15, bf16[512,1024]{1,0:T(8,128)(2,1)} %all-gather.6.cloned.1.call-done), kind=kOutput, calls=%fused_computation.15 | convolution fusion | flops 4297064448 | bytes 13631488 | tf_op jit(solution)/shard_map/dot_general | solution.py:18
  56.3 6.5 %fusion.7 = bf16[512,4096]{0,1:T(8,128)(2,1)} fusion(bf16[1024,4096]{0,1:T(8,128)(2,1)S(1)} %copy-done.1, bf16[512,1024]{1,0:T(8,128)(2,1)S(1)} %copy-done.5), kind=kOutput, calls=%fused_computation.16 | convolution fusion | flops 4297064448 | bytes 13631488 | tf_op jit(solution)/shard_map/dot_general | solution.py:18
  62.8 6.4 %all-gather.8.cloned.1.call-done = bf16[512,1024]{1,0:T(8,128)(2,1)} async-done(((bf16[128,1024]{1,0:T(8,128)(2,1)}), bf16[512,1024]{1,0:T(8,128)(2,1)}) %all-gather.8.cloned.1.call-update) | async-done | bytes 1048592 | tf_op jit(solution)/shard_map/all_gather | solution.py:40
  69.4 11.7 %broadcast_in_dim.21 = bf16[4096,8,128]{2,1,0:T(8,128)(2,1)S(1)} broadcast(bf16[4096,8]{1,0:T(8,128)(2,1)S(1)} %bitcast.53), dimensions={0,1} | broadcast | bytes 8454144 | tf_op jit(solution)/shard_map/broadcast_in_dim | solution.py:14
  81.2 12.6 %fusion.5 = bf16[512,4096]{0,1:T(8,128)(2,1)} fusion(bf16[512,1024]{1,0:T(8,128)(2,1)S(1)} %copy-done.3, bf16[4096,1024]{1,0:T(8,128)(2,1)} %param.11, bf16[512,8,8,128]{3,2,1,0:T(8,128)(2,1)S(1)} %bitcast.51), kind=kOutput, calls=%fused_computation.14 | convolution fusion | flops 4301258752 | bytes 22020096 | tf_op jit(solution)/shard_map/dot_general | solution.py:22
  93.8 22.0 %pad_maximum_fusion = bf16[512,12288]{0,1:T(8,128)(2,1)} fusion(bf16[512,4096]{0,1:T(8,128)(2,1)} %fusion.5, bf16[512,4096]{0,1:T(8,128)(2,1)} %fusion.7, bf16[512,4096]{0,1:T(8,128)(2,1)S(1)} %copy-done.2), kind=kLoop, calls=%fused_computation.7 | loop fusion | flops 37748736 | bytes 25165824 | tf_op jit(solution)/shard_map/concatenate | solution.py:49
  115.8 16.7 %copy.23 = bf16[512,12288]{1,0:T(8,128)(2,1)} copy(bf16[512,12288]{0,1:T(8,128)(2,1)} %pad_maximum_fusion) | data formatting | bytes 25165824
  132.6 98.6 %reduce-scatter.7.cloned.1.call-done = bf16[128,12288]{1,0:T(8,128)(2,1)} async-done(((bf16[512,12288]{1,0:T(8,128)(2,1)}), bf16[128,12288]{1,0:T(8,128)(2,1)}) %reduce-scatter.7.cloned.1.call-update) | async-done | bytes 3145744
  231.2 3.5 copy.24
  235.2 2.8 multiply_convert_fusion.1
  239.2 34.0 %all-gather.10.cloned.1.call-done = bf16[512,4096]{0,1:T(8,128)(2,1)} async-done(((bf16[128,4096]{0,1:T(8,128)(2,1)}), bf16[512,4096]{0,1:T(8,128)(2,1)}) %all-gather.10.cloned.1.call-update) | async-done | bytes 4194320 | tf_op jit(solution)/shard_map/all_gather | solution.py:69
  273.2 8.2 %fusion.8 = f32[512,1024]{1,0:T(8,128)S(1)} fusion(bf16[512,4096]{0,1:T(8,128)(2,1)} %all-gather.10.cloned.1.call-done, bf16[1024,4096]{0,1:T(8,128)(2,1)} %get-tuple-element.15), kind=kOutput, calls=%fused_computation.23 | convolution fusion | flops 4294967296 | bytes 14680064 | tf_op jit(solution)/shard_map/dot_general | solution.py:22
  281.4 28.2 %all-gather.12.cloned.1.call-done = bf16[512,4096]{0,1:T(8,128)(2,1)} async-done(((bf16[128,4096]{0,1:T(8,128)(2,1)}), bf16[512,4096]{0,1:T(8,128)(2,1)}) %all-gather.12.cloned.1.call-update) | async-done | bytes 4194320 | tf_op jit(solution)/shard_map/all_gather | solution.py:70
  309.6 10.2 %add_convert_fusion = bf16[512,1024]{1,0:T(8,128)(2,1)} fusion(f32[512,1024]{1,0:T(8,128)S(1)} %fusion.8, bf16[512,4096]{0,1:T(8,128)(2,1)} %all-gather.12.cloned.1.call-done, bf16[1024,4096]{0,1:T(8,128)(2,1)} %get-tuple-element.16), kind=kOutput, calls=%fused_computation.18 | convolution fusion | flops 4296015872 | bytes 15728640 | tf_op jit(solution)/shard_map/dot_general | solution.py:22
  319.8 9.0 %fusion.1 = bf16[1024,4096]{0,1:T(8,128)(2,1)} fusion(bf16[512,4096]{0,1:T(8,128)(2,1)} %all-gather.12.cloned.1.call-done, bf16[512,1024]{1,0:T(8,128)(2,1)S(1)} %copy-done.6, bf16[1024,32]{0,1:T(8,128)(2,1)S(1)} %bitcast.55), kind=kOutput, calls=%fused_computation.5 | convolution fusion | flops 4307550208 | bytes 13697024 | tf_op jit(solution)/shard_map/dot_general | solution.py:26
  328.9 11.9 %copy.22 = bf16[1024,4096]{1,0:T(8,128)(2,1)} copy(bf16[1024,4096]{0,1:T(8,128)(2,1)} %fusion.1) | data formatting | bytes 16777216
  340.8 8.9 %fusion = bf16[1024,4096]{0,1:T(8,128)(2,1)} fusion(bf16[512,4096]{0,1:T(8,128)(2,1)} %all-gather.10.cloned.1.call-done, bf16[512,1024]{1,0:T(8,128)(2,1)S(1)} %copy-done.6, bf16[1024,32]{0,1:T(8,128)(2,1)S(1)} %bitcast.56), kind=kOutput, calls=%fused_computation.4 | convolution fusion | flops 4307550208 | bytes 13697024 | tf_op jit(solution)/shard_map/dot_general | solution.py:26
  349.7 12.0 %copy.21 = bf16[1024,4096]{1,0:T(8,128)(2,1)} copy(bf16[1024,4096]{0,1:T(8,128)(2,1)} %fusion) | data formatting | bytes 16777216
  361.7 12.7 %multiply_convert_fusion = bf16[4096,1024]{1,0:T(8,128)(2,1)} fusion(bf16[512,8,8,128]{3,2,1,0:T(8,128)(2,1)} %bitcast.52, bf16[512,4096]{0,1:T(8,128)(2,1)} %all-gather.14.cloned.1.call-done, bf16[512,1024]{1,0:T(8,128)(2,1)S(1)} %copy-done.4), kind=kOutput, calls=%fused_computation.6 | convolution fusion | flops 4307550208 | bytes 22020096 | tf_op jit(solution)/shard_map/dot_general | solution.py:26
  374.3 1.8 reduce-scatter.5.cloned.1.call-done
  (37 shorter events, 4.4 us)
Async XLA Ops:
  7.2 38.7 %all-gather.6.cloned.1.call-start = ((), (), s32[]{:S(2)}) async-start(), calls=%async_computation.2 | async-start | bytes 1310720 | tf_op jit(solution)/shard_map/all_gather | solution.py:39
  7.9 61.4 %all-gather.8.cloned.1.call-start = ((), (), s32[]{:S(2)}) async-start(), calls=%async_computation.3 | async-start | bytes 1310720 | tf_op jit(solution)/shard_map/all_gather | solution.py:40
  8.6 222.6 %reduce-scatter.7.cloned.1.call-start = ((), (), s32[]{:S(2)}) async-start(), calls=%async_computation.8 | async-start | bytes 15728640
  45.8 10.5 %copy-start.1 = (bf16[1024,4096]{0,1:T(8,128)(2,1)S(1)}, bf16[1024,4096]{0,1:T(8,128)(2,1)}, u32[]{:S(2)}) copy-start(bf16[1024,4096]{0,1:T(8,128)(2,1)} %get-tuple-element.16) | copy-start | bytes 25165828
  45.8 10.5 %copy-start.5 = (bf16[512,1024]{1,0:T(8,128)(2,1)S(1)}, bf16[512,1024]{1,0:T(8,128)(2,1)}, u32[]{:S(2)}) copy-start(bf16[512,1024]{1,0:T(8,128)(2,1)} %all-gather.6.cloned.1.call-done) | copy-start | bytes 3145732
  69.3 11.9 %copy-start.3 = (bf16[512,1024]{1,0:T(8,128)(2,1)S(1)}, bf16[512,1024]{1,0:T(8,128)(2,1)}, u32[]{:S(2)}) copy-start(bf16[512,1024]{1,0:T(8,128)(2,1)} %all-gather.8.cloned.1.call-done) | copy-start | bytes 3145732
  81.1 12.6 %copy-start = (bf16[4096,8,128]{2,1,0:T(8,128)(2,1)}, bf16[4096,8,128]{2,1,0:T(8,128)(2,1)S(1)}, u32[]{:S(2)}) copy-start(bf16[4096,8,128]{2,1,0:T(8,128)(2,1)S(1)} %broadcast_in_dim.21) | copy-start | bytes 25165828
  81.2 12.6 %copy-start.2 = (bf16[512,4096]{0,1:T(8,128)(2,1)S(1)}, bf16[512,4096]{0,1:T(8,128)(2,1)}, u32[]{:S(2)}) copy-start(bf16[512,4096]{0,1:T(8,128)(2,1)} %fusion.6) | copy-start | bytes 12582916
  132.5 140.6 %all-gather.10.cloned.1.call-start = ((), (), s32[]{:S(2)}) async-start(), calls=%async_computation.4 | async-start | bytes 5242880 | tf_op jit(solution)/shard_map/all_gather | solution.py:69
  238.0 71.6 %all-gather.12.cloned.1.call-start = ((), (), s32[]{:S(2)}) async-start(), calls=%async_computation.5 | async-start | bytes 5242880 | tf_op jit(solution)/shard_map/all_gather | solution.py:70
  238.6 123.1 %all-gather.14.cloned.1.call-start = ((), (), s32[]{:S(2)}) async-start(), calls=%async_computation.7 | async-start | bytes 5242880 | tf_op jit(solution)/shard_map/all_gather | solution.py:68
  239.2 137.0 %reduce-scatter.5.cloned.1.call-start = ((), (), s32[]{:S(2)}) async-start(), calls=%async_computation.6 | async-start | bytes 1310720 | tf_op jit(solution)/shard_map/reduce_scatter | solution.py:75
  281.4 38.4 %copy-start.6 = (bf16[512,1024]{1,0:T(8,128)(2,1)S(1)}, bf16[512,1024]{1,0:T(8,128)(2,1)}, u32[]{:S(2)}) copy-start(bf16[512,1024]{1,0:T(8,128)(2,1)} %all-gather.6.cloned.1.call-done) | copy-start | bytes 3145732
  349.7 12.0 %copy-start.4 = (bf16[512,1024]{1,0:T(8,128)(2,1)S(1)}, bf16[512,1024]{1,0:T(8,128)(2,1)}, u32[]{:S(2)}) copy-start(bf16[512,1024]{1,0:T(8,128)(2,1)} %all-gather.8.cloned.1.call-done) | copy-start | bytes 3145732
Sparse Core Ops, SparseCore 0:
  9.6 30.6 all-gather.5
  41.8 27.4 all-gather.7
  132.7 98.5 reduce-scatter.6
  238.1 35.0 all-gather.9
  274.6 35.0 all-gather.11
  311.0 35.0 all-gather.13
  349.0 27.1 reduce-scatter.4
where the time goes:
time: 385 us; the launch traced here: 383 us
  waiting for transfers between devices  172 us (45%)
  local copies, waits for them, and re-layouts  80.2 us (21%)
  matrix products  78.6 us (20%)
  other arithmetic  38.1 us (10%)
  between operations  14.2 us (4%)
    unnamed x8, waiting for transfers between devices  101 us
    unnamed x21, local copies, waits for them, and re-layouts  68.1 us
    all_gather x1, waiting for transfers between devices, on_device(): lax.all_gather(gate_delta, 'row', axis=0, tiled=True)  34 us
    dot_general x3, matrix products, dense_behind(): lax.dot_general(left, weight, CONTRACT_COLUMNS, preferred_element_type=jn...  31 us
    dot_general x3, matrix products, dense_outer(): lax.dot_general(left, right, CONTRACT_ROWS, preferred_element_type=jnp.fl...  30.6 us
    all_gather x1, waiting for transfers between devices, on_device(): lax.all_gather(up_delta, 'row', axis=0, tiled=True)  28.2 us
    concatenate x1, other arithmetic, on_device(): jnp.concatenate([jnp.concatenate([dense_ahead(token_rows, gate_kept), den...  22 us
    dot_general x2, matrix products, dense_ahead(): return jnp.dot(left, weight, preferred_element_type=jnp.float32)  17 us
  transfers between devices with their start and end apart: 7, of which 5 were waited for; matrix products, arithmetic and copies ran while one was open for 33% of the time, Pallas kernels for 0%

commit v1 on v0

v1 whole, which is shorter than its diff:
```python
import functools

import jax
import jax.numpy as jnp
from jax import lax
from jax.experimental import pallas as pl
from jax.experimental.pallas import tpu as pltpu
from jax.sharding import PartitionSpec as P

BLK = 128
CONTRACT_ROWS = (((0,), (0,)), ((), ()))
CONTRACT_COLUMNS = (((1,), (1,)), ((), ()))


def widen(keep, axis):
    return jnp.repeat(keep, BLK, axis=axis).astype(jnp.bfloat16)


def masked(weight, lines):
    rows, columns = weight.shape
    blocked = weight.reshape(rows // BLK, BLK, columns) * lines[:, None, :]
    return blocked.reshape(rows, columns)


def ahead(left, weight):
    return jnp.dot(left, weight, preferred_element_type=jnp.float32)


def behind(left, weight):
    return lax.dot_general(left, weight, CONTRACT_COLUMNS, preferred_element_type=jnp.float32)


def outer(left, right):
    return lax.dot_general(left, right, CONTRACT_ROWS, preferred_element_type=jnp.float32)


def deltas(total):
    gate, up, hidden_delta = total[0], total[1], total[2]
    sigma = jax.nn.sigmoid(gate)
    active = gate * sigma
    hidden = active * up
    gate_delta = hidden_delta * up * sigma * (1.0 + gate * (1.0 - sigma))
    up_delta = hidden_delta * active
    return jnp.stack([hidden, gate_delta, up_delta]).astype(jnp.bfloat16)


def gradient_kernel(flip, left_ref, right_ref, mask_ref, *refs):
    out_ref = refs[-1]
    if flip:
        product = outer(left_ref[...], right_ref[...])
    else:
        product = ahead(left_ref[...], right_ref[...])
    rows, columns = product.shape
    blocked = product.reshape(rows // BLK, BLK, columns) * mask_ref[...].reshape(rows // BLK, 1, columns)
    out_ref[...] = blocked.reshape(rows, columns).astype(out_ref.dtype)


def column_gradient(rows_t, delta, mask, into, shape, first):
    height, depth = rows_t.shape
    width = delta.shape[1]
    step = min(256, width)
    base = first // step
    extra = [] if into is None else [into]
    return pl.pallas_call(
        functools.partial(gradient_kernel, False),
        out_shape=jax.ShapeDtypeStruct(shape, jnp.bfloat16),
        grid=(width // step,),
        in_specs=[
            pl.BlockSpec((height, depth), lambda j: (0, 0)),
            pl.BlockSpec((depth, step), lambda j: (0, j)),
            pl.BlockSpec((height // BLK, step), lambda j: (0, base + j)),
        ]
        + [pl.BlockSpec(memory_space=pl.ANY)] * len(extra),
        out_specs=pl.BlockSpec((height, step), lambda j: (0, base + j)),
        input_output_aliases={3: 0} if extra else {},
        compiler_params=pltpu.CompilerParams(vmem_limit_bytes=24 * 2**20),
        cost_estimate=pl.CostEstimate(
            flops=2 * height * depth * width, bytes_accessed=2 * height * width, transcendentals=0
        ),
    )(rows_t, delta, mask, *extra)


def line_gradient(hidden, rows, mask, into, shape, first):
    depth, width = hidden.shape
    breadth = rows.shape[1]
    step = min(256, width)
    base = first // step
    extra = [] if into is None else [into]
    return pl.pallas_call(
        functools.partial(gradient_kernel, True),
        out_shape=jax.ShapeDtypeStruct(shape, jnp.bfloat16),
        grid=(width // step,),
        in_specs=[
            pl.BlockSpec((depth, step), lambda j: (0, j)),
            pl.BlockSpec((depth, breadth), lambda j: (0, 0)),
            pl.BlockSpec((step // BLK, 1, breadth), lambda j: (base + j, 0, 0)),
        ]
        + [pl.BlockSpec(memory_space=pl.ANY)] * len(extra),
        out_specs=pl.BlockSpec((step, breadth), lambda j: (base + j, 0)),
        input_output_aliases={3: 0} if extra else {},
        compiler_params=pltpu.CompilerParams(vmem_limit_bytes=24 * 2**20),
        cost_estimate=pl.CostEstimate(
            flops=2 * depth * width * breadth, bytes_accessed=2 * width * breadth, transcendentals=0
        ),
    )(hidden, rows, mask[:, None, :], *extra)


def on_device(n_row, n_col, tokens, cotangent, gate_weight, up_weight, down_weight, gate_keep, down_keep):
    core = lax.rem(lax.axis_index("row"), 2)
    chips = n_row // 2
    swap = [(i, i ^ 1) for i in range(n_row)]
    height, width = gate_weight.shape
    own_rows = tokens.shape[0]
    size = min(1024, width)
    chunks = width // size

    def across(value):
        total = value.astype(jnp.float32)
        for k in range(1, chips):
            pairs = [(i, (i + 2 * k) % n_row) for i in range(n_row)]
            total = total + lax.ppermute(value, "row", pairs).astype(jnp.float32)
        return total

    def core_order(value):
        half = value.shape[1] // 2
        mine = lax.dynamic_slice_in_dim(value, core * half, half, 1)
        theirs = lax.dynamic_slice_in_dim(value, (1 - core) * half, half, 1)
        return jnp.concatenate([mine, theirs], axis=1)

    both = jnp.stack([tokens, cotangent])
    blocks = []
    for s in range(1, n_col):
        blocks.append(lax.ppermute(both, "col", [(i, (i + s) % n_col) for i in range(n_col)]))
    own = core_order(both)
    groups = [own]
    if blocks:
        groups.append(jnp.concatenate([core_order(b)[:, : own_rows // 2] for b in blocks] + [core_order(b)[:, own_rows // 2 :] for b in blocks], axis=1))
    rows = jnp.concatenate(groups, axis=1)
    tokens_t = rows[0].T

    gate_lines = widen(gate_keep, 1)
    down_lines = widen(down_keep, 1)
    gate_lines_wide = gate_lines.astype(jnp.float32)
    down_lines_wide = down_lines.astype(jnp.float32)

    weights = []
    for k in range(chunks):
        lower = k * size
        lines = gate_lines[:, lower : lower + size]
        weights.append(
            (
                masked(gate_weight[:, lower : lower + size], lines),
                masked(up_weight[:, lower : lower + size], lines),
                masked(down_weight[lower : lower + size], down_lines[lower // BLK : (lower + size) // BLK]),
            )
        )

    def unit(g, k):
        x, (gate, up, down) = groups[g], weights[k]
        half = x.shape[1] // 2
        whole = jnp.stack([ahead(x[0], gate), ahead(x[0], up), behind(x[1], down)]).astype(jnp.bfloat16)
        came = lax.ppermute(whole[:, half:], "row", swap)
        mine = (whole[:, :half].astype(jnp.float32) + came.astype(jnp.float32)).astype(jnp.bfloat16)
        result = deltas(across(mine))
        return jnp.concatenate([result, lax.ppermute(result, "row", swap)], axis=1)

    early = max(1, chunks - 1)
    order = [(0, k) for k in range(early)] + [(g, k) for g in range(1, len(groups)) for k in range(chunks)] + [(0, k) for k in range(early, chunks)]
    outs = {}
    for g, k in order:
        outs[g, k] = unit(g, k)

    gate_gradient = up_gradient = down_gradient = None
    terms = [0.0] * len(groups)
    for k in range(chunks):
        gate, up, down = weights[k]
        for g in range(len(groups)):
            terms[g] = terms[g] + behind(outs[g, k][1], gate) + behind(outs[g, k][2], up)
        h = jnp.concatenate([outs[g, k] for g in range(len(groups))], axis=1)
        gate_gradient = column_gradient(tokens_t, h[1], gate_lines_wide, gate_gradient, gate_weight.shape, k * size)
        up_gradient = column_gradient(tokens_t, h[2], gate_lines_wide, up_gradient, up_weight.shape, k * size)
        down_gradient = line_gradient(h[0], rows[1], down_lines_wide, down_gradient, down_weight.shape, k * size)

    total = terms[0]
    half = own_rows // 2
    if blocks:
        other = terms[1].astype(jnp.bfloat16)
        middle = half * len(blocks)
        for s in range(1, n_col):
            at = (s - 1) * half
            block = jnp.concatenate([other[at : at + half], other[middle + at : middle + at + half]], axis=0)
            total = total + lax.ppermute(block, "col", [(i, (i - s) % n_col) for i in range(n_col)]).astype(jnp.float32)
    restored = core_order(total[None])[0]
    return (restored.astype(jnp.bfloat16), gate_gradient, up_gradient, down_gradient)


def solution(mesh):
    placed = (
        P(("groups", "col"), "row"),
        P(("groups", "col"), "row"),
        P("row", "col"),
        P("row", "col"),
        P("col", "row"),
        P("row", "col"),
        P("col", "row"),
    )
    return jax.shard_map(
        functools.partial(on_device, mesh.shape["row"], mesh.shape["col"]),
        mesh=mesh,
        in_specs=placed,
        out_specs=(
            P(("groups", "col"), "row"),
            P(("groups", "row"), "col"),
            P(("groups", "row"), "col"),
            P(("groups", "col"), "row"),
        ),
        check_vma=False,
    )
```

time: 385 us -> 274 us (0.71)
  waiting for transfers between devices: 172 us -> 93.4 us
  local copies, waits for them, and re-layouts: 80.2 us -> 29.6 us
  matrix products: 78.6 us -> 37.3 us
  Pallas kernels: 0 us -> 36.8 us
  starting transfers between devices: 0.27 us -> 23.6 us
  between operations: 14.2 us -> 2.26 us
  other arithmetic: 38.1 us -> 46.8 us
    unnamed x8 -> x0, waiting for transfers between devices: 101 us -> none
    ppermute x0 -> x30, waiting for transfers between devices: none -> 93.4 us  [the longest x8 93.3 us: across(): total = total + lax.ppermute(value, 'row', pairs).astype(jnp.float32)]
    all_gather x5 -> x0, waiting for transfers between devices: 68.6 us -> none  [the longest x1 34 us: on_device(): lax.all_gather(gate_delta, 'row', axis=0, tiled=True)]
    unnamed x21 -> x105, local copies, waits for them, and re-layouts: 68.1 us -> 17.4 us
    dot_general x8 -> x40, matrix products: 78.6 us -> 37.3 us  [the longest x24 24.6 us: behind(): lax.dot_general(left, weight, CONTRACT_COLUMNS, preferred_element_type=jn...]
    pallas_call x0 -> x12, Pallas kernels: none -> 36.8 us  [the longest x8 24.3 us: column_gradient(): pl.pallas_call(functools.partial(gradient_kernel, False), out_shape=jax.S...]
    ppermute x0 -> x30, starting transfers between devices: none -> 23.6 us  [the longest x8 8.57 us: across(): total = total + lax.ppermute(value, 'row', pairs).astype(jnp.float32)]
    concatenate x1 -> x7, other arithmetic: 22 us -> 2.88 us  [the longest x4 2.83 us: on_device(): h = jnp.concatenate([outs[g, k] for g in range(len(groups))], axis=1)]
  transfers between devices with their start and end apart: 7 -> 30, of which waited for: 5 -> 4; matrix products, arithmetic and copies ran while one was open for 33% -> 35% of each run, Pallas kernels for 0% -> 14%
where the time goes in v1:
time: 274 us; the launch traced here: 270 us
  waiting for transfers between devices  93.4 us (34%)
  other arithmetic  46.8 us (17%)
  matrix products  37.3 us (14%)
  Pallas kernels  36.8 us (13%)
  local copies, waits for them, and re-layouts  29.6 us (11%)
  starting transfers between devices  23.6 us (9%)
    ppermute x8, waiting for transfers between devices, across(): total = total + lax.ppermute(value, 'row', pairs).astype(jnp.float32)  93.3 us
    dot_general x24, matrix products, behind(): lax.dot_general(left, weight, CONTRACT_COLUMNS, preferred_element_type=jn...  24.6 us
    pallas_call x8, Pallas kernels, column_gradient(): pl.pallas_call(functools.partial(gradient_kernel, False), out_shape=jax.S...  24.3 us
    unnamed x105, local copies, waits for them, and re-layouts  17.4 us
    mul x2, other arithmetic, masked(): blocked = weight.reshape(rows // BLK, BLK, columns) * lines[:, None, :]  15.1 us
    dot_general x16, matrix products, ahead(): return jnp.dot(left, weight, preferred_element_type=jnp.float32)  12.7 us
    pallas_call x4, Pallas kernels, line_gradient(): pl.pallas_call(functools.partial(gradient_kernel, True), out_shape=jax.Sh...  12.5 us
    convert_element_type x8, other arithmetic, unit(): (whole[:, :half].astype(jnp.float32) + came.astype(jnp.float32)).astype(j...  8.9 us
  transfers between devices with their start and end apart: 30, of which 4 were waited for; matrix products, arithmetic and copies ran while one was open for 35% of the time, Pallas kernels for 14%

profile of v1, /device:TPU:0, one launch (start us, length us, event | category | flops | bytes accessed | tf_op | source)
XLA Modules:
  0.0 269.7 jit_solution(4150969635475970696)
XLA Ops:
  2.6 3.0 %collective-permute-start.12 = (bf16[2,128,1024]{2,1,0:T(8,128)(2,1)}, bf16[2,128,1024]{2,1,0:T(8,128)(2,1)}, u32[]{:S(2)}, u32[]{:S(2)}) collective-permute-start(bf16[2,128,1024]{2,1,0:T(8,128)(2,1)} %pad_maximum_fusion.36), channel_id=1, source_target_pairs={{0,1},{1,2},{2,3},{3,0},{4,5},{5,6},{6,7},{7,4},{8,9},{9,10},{10,1... | collective-permute-start | bytes 1572872 | tf_op jit(solution)/shard_map/ppermute | solution.py:133
  5.6 2.6 collective-permute-start.13
  13.1 6.7 %bitcast_multiply_fusion.6 = (bf16[1024,1024]{1,0:T(8,128)(2,1)S(1)}, bf16[1024,1024]{1,0:T(8,128)(2,1)S(1)}, bf16[1024,1024]{1,0:T(8,128)(2,1)S(1)}, bf16[1024,...) fusion(bf16[1024,4096]{1,0:T(8,128)(2,1)} %param.10, ...), kind=kLoop, calls=%fused_computation.10 | loop fusion | flops 8388608 | bytes 33619968 | tf_op jit(solution)/shard_map/mul | solution.py:21
  20.9 8.4 %bitcast_multiply_fusion.11 = (bf16[1024,1024]{1,0:T(8,128)(2,1)S(1)}, bf16[1024,1024]{1,0:T(8,128)(2,1)S(1)}, bf16[1024,1024]{1,0:T(8,128)(2,1)S(1)}, bf16[1024,1024]{1,0:T(8,128)(2,1)S(1)}) fusion(bf16[4096,1024]{1,0:T(8,128)(2,1)} %param.11, bf16[8,1024]{1,0:T(8,128)(2,1)S(1)} %get-tuple-element.97, bf16[8,1024]{1,0:T(8,128)(2,1)S(1)} %get-tuple-element.96, ...), kind=kLoop, calls=%fused_computation.27 | loop fusion | flops 4194304 | bytes 16842752 | tf_op jit(solution)/shard_map/mul | solution.py:21
  43.2 2.0 add_convert_fusion.5
  112.0 21.7 %collective-permute-done.25 = bf16[3,192,1024]{2,1,0:T(8,128)(2,1)S(1)} collective-permute-done((bf16[3,192,1024]{2,1,0:T(8,128)(2,1)S(1)}, bf16[3,192,1024]{2,1,0:T(8,128)(2,1)S(1)}, u32[]{:S(2)}, u32[]{:S(2)}) %collective-permute-start.25) | collective-permute-done | bytes 1179680 | tf_op jit(solution)/shard_map/ppermute | solution.py:121
  134.9 24.0 %collective-permute-done.22 = bf16[3,192,1024]{2,1,0:T(8,128)(2,1)S(1)} collective-permute-done((bf16[3,192,1024]{2,1,0:T(8,128)(2,1)S(1)}, bf16[3,192,1024]{2,1,0:T(8,128)(2,1)S(1)}, u32[]{:S(2)}, u32[]{:S(2)}) %collective-permute-start.22) | collective-permute-done | bytes 1179680 | tf_op jit(solution)/shard_map/ppermute | solution.py:121
  160.2 24.0 %collective-permute-done.19 = bf16[3,192,1024]{2,1,0:T(8,128)(2,1)S(1)} collective-permute-done((bf16[3,192,1024]{2,1,0:T(8,128)(2,1)S(1)}, bf16[3,192,1024]{2,1,0:T(8,128)(2,1)S(1)}, u32[]{:S(2)}, u32[]{:S(2)}) %collective-permute-start.19) | collective-permute-done | bytes 1179680 | tf_op jit(solution)/shard_map/ppermute | solution.py:121
  185.5 23.6 %collective-permute-done.16 = bf16[3,192,1024]{2,1,0:T(8,128)(2,1)S(1)} collective-permute-done((bf16[3,192,1024]{2,1,0:T(8,128)(2,1)S(1)}, bf16[3,192,1024]{2,1,0:T(8,128)(2,1)S(1)}, u32[]{:S(2)}, u32[]{:S(2)}) %collective-permute-start.16) | collective-permute-done | bytes 1179680 | tf_op jit(solution)/shard_map/ppermute | solution.py:121
  215.1 2.0 fusion.72
  217.1 2.0 fusion.69
  222.4 2.2 collective-permute-start.28
  230.8 3.0 %shard_map.102.refs_0_ = bf16[1024,4096]{1,0:T(8,128)(2,1)} custom-call(bf16[1024,512]{1,0:T(8,128)(2,1)S(1)} %copy.24.left_ref, bf16[512,1024]{1,0:T(8,128)(2,1)S(1)} %get-tuple-element.22.right_ref, f32[8,4096]{1,0:T(8,128)S(1)} %get-tuple-element.88.mask_ref), custom_call_target="tpu_custom_call" | custom-call | flops 1073741824 | bytes 2097152 | tf_op jit(solution)/shard_map/pallas_call | solution.py:64
  233.8 3.0 %shard_map.106.refs_0_ = bf16[1024,4096]{1,0:T(8,128)(2,1)} custom-call(bf16[1024,512]{1,0:T(8,128)(2,1)S(1)} %copy.24.left_ref, bf16[512,1024]{1,0:T(8,128)(2,1)S(1)} %get-tuple-element.21.right_ref, f32[8,4096]{1,0:T(8,128)S(1)} %get-tuple-element.88.mask_ref), custom_call_target="tpu_custom_call" | custom-call | flops 1073741824 | bytes 2097152 | tf_op jit(solution)/shard_map/pallas_call | solution.py:64
  236.9 3.0 %shard_map.103.refs_0_ = bf16[1024,4096]{1,0:T(8,128)(2,1)} custom-call(bf16[1024,512]{1,0:T(8,128)(2,1)S(1)} %copy.24.left_ref, bf16[512,1024]{1,0:T(8,128)(2,1)S(1)} %get-tuple-element.25.right_ref, f32[8,4096]{1,0:T(8,128)S(1)} %get-tuple-element.88.mask_ref, bf16[1024,4096]{1,0:T(8,128)(2,1)} %shard_map.102.refs_0_), custom_call_target="tpu_custom_call", output_to_operand_aliasing={{}: (3, {})} | custom-call | flops 1073741824 | bytes 2097152 | tf_op jit(solution)/shard_map/pallas_call | solution.py:64
  239.9 3.0 %shard_map.104.refs_0_ = bf16[1024,4096]{1,0:T(8,128)(2,1)} custom-call(bf16[1024,512]{1,0:T(8,128)(2,1)S(1)} %copy.24.left_ref, bf16[512,1024]{1,0:T(8,128)(2,1)S(1)} %get-tuple-element.28.right_ref, f32[8,4096]{1,0:T(8,128)S(1)} %get-tuple-element.88.mask_ref, bf16[1024,4096]{1,0:T(8,128)(2,1)} %shard_map.103.refs_0_), custom_call_target="tpu_custom_call", output_to_operand_aliasing={{}: (3, {})} | custom-call | flops 1073741824 | bytes 2097152 | tf_op jit(solution)/shard_map/pallas_call | solution.py:64
  242.9 3.0 %shard_map.105 = bf16[1024,4096]{1,0:T(8,128)(2,1)} custom-call(bf16[1024,512]{1,0:T(8,128)(2,1)S(1)} %copy.24.left_ref, bf16[512,1024]{1,0:T(8,128)(2,1)S(1)} %get-tuple-element.31.right_ref, f32[8,4096]{1,0:T(8,128)S(1)} %get-tuple-element.88.mask_ref, bf16[1024,4096]{1,0:T(8,128)(2,1)} %shard_map.104.refs_0_), custom_call_target="tpu_custom_call", output_to_operand_aliasing={{}: (3, {})} | custom-call | flops 1073741824 | bytes 2097152 | tf_op jit(solution)/shard_map/pallas_call | solution.py:64
  246.0 3.0 %shard_map.107.refs_0_ = bf16[1024,4096]{1,0:T(8,128)(2,1)} custom-call(bf16[1024,512]{1,0:T(8,128)(2,1)S(1)} %copy.24.left_ref, bf16[512,1024]{1,0:T(8,128)(2,1)S(1)} %get-tuple-element.24.right_ref, f32[8,4096]{1,0:T(8,128)S(1)} %get-tuple-element.88.mask_ref, bf16[1024,4096]{1,0:T(8,128)(2,1)} %shard_map.106.refs_0_), custom_call_target="tpu_custom_call", output_to_operand_aliasing={{}: (3, {})} | custom-call | flops 1073741824 | bytes 2097152 | tf_op jit(solution)/shard_map/pallas_call | solution.py:64
  249.0 3.0 %shard_map.108.refs_0_ = bf16[1024,4096]{1,0:T(8,128)(2,1)} custom-call(bf16[1024,512]{1,0:T(8,128)(2,1)S(1)} %copy.24.left_ref, bf16[512,1024]{1,0:T(8,128)(2,1)S(1)} %get-tuple-element.27.right_ref, f32[8,4096]{1,0:T(8,128)S(1)} %get-tuple-element.88.mask_ref, bf16[1024,4096]{1,0:T(8,128)(2,1)} %shard_map.107.refs_0_), custom_call_target="tpu_custom_call", output_to_operand_aliasing={{}: (3, {})} | custom-call | flops 1073741824 | bytes 2097152 | tf_op jit(solution)/shard_map/pallas_call | solution.py:64
  252.1 3.0 %shard_map.109 = bf16[1024,4096]{1,0:T(8,128)(2,1)} custom-call(bf16[1024,512]{1,0:T(8,128)(2,1)S(1)} %copy.24.left_ref, bf16[512,1024]{1,0:T(8,128)(2,1)S(1)} %get-tuple-element.30.right_ref, f32[8,4096]{1,0:T(8,128)S(1)} %get-tuple-element.88.mask_ref, bf16[1024,4096]{1,0:T(8,128)(2,1)} %shard_map.108.refs_0_), custom_call_target="tpu_custom_call", output_to_operand_aliasing={{}: (3, {})} | custom-call | flops 1073741824 | bytes 2097152 | tf_op jit(solution)/shard_map/pallas_call | solution.py:64
  255.2 3.1 %shard_map.110.refs_0_ = bf16[4096,1024]{1,0:T(8,128)(2,1)} custom-call(bf16[512,1024]{1,0:T(8,128)(2,1)S(1)} %get-tuple-element.20.left_ref, bf16[512,1024]{1,0:T(8,128)(2,1)S(1)} %get-tuple-element.44.right_ref, f32[32,1,1024]{2,1,0:T(1,128)S(1)} %bitcast.240), custom_call_target="tpu_custom_call" | custom-call | flops 1073741824 | bytes 2097152 | tf_op jit(solution)/shard_map/pallas_call | solution.py:89
  258.3 3.1 %shard_map.111.refs_0_ = bf16[4096,1024]{1,0:T(8,128)(2,1)} custom-call(bf16[512,1024]{1,0:T(8,128)(2,1)S(1)} %get-tuple-element.23.left_ref, bf16[512,1024]{1,0:T(8,128)(2,1)S(1)} %get-tuple-element.44.right_ref, f32[32,1,1024]{2,1,0:T(1,128)S(1)} %bitcast.241, bf16[4096,1024]{1,0:T(8,128)(2,1)} %shard_map.110.refs_0_), custom_call_target="tpu_custom_call", output_to_operand_aliasing={{}: (3, {})} | custom-call | flops 1073741824 | bytes 2097152 | tf_op jit(solution)/shard_map/pallas_call | solution.py:89
  261.4 3.1 %shard_map.112.refs_0_ = bf16[4096,1024]{1,0:T(8,128)(2,1)} custom-call(bf16[512,1024]{1,0:T(8,128)(2,1)S(1)} %get-tuple-element.26.left_ref, bf16[512,1024]{1,0:T(8,128)(2,1)S(1)} %get-tuple-element.44.right_ref, f32[32,1,1024]{2,1,0:T(1,128)S(1)} %bitcast.242, bf16[4096,1024]{1,0:T(8,128)(2,1)} %shard_map.111.refs_0_), custom_call_target="tpu_custom_call", output_to_operand_aliasing={{}: (3, {})} | custom-call | flops 1073741824 | bytes 2097152 | tf_op jit(solution)/shard_map/pallas_call | solution.py:89
  264.5 3.1 %shard_map.113 = bf16[4096,1024]{1,0:T(8,128)(2,1)} custom-call(bf16[512,1024]{1,0:T(8,128)(2,1)S(1)} %get-tuple-element.29.left_ref, bf16[512,1024]{1,0:T(8,128)(2,1)S(1)} %get-tuple-element.44.right_ref, f32[32,1,1024]{2,1,0:T(1,128)S(1)} %bitcast.243, bf16[4096,1024]{1,0:T(8,128)(2,1)} %shard_map.112.refs_0_), custom_call_target="tpu_custom_call", output_to_operand_aliasing={{}: (3, {})} | custom-call | flops 1073741824 | bytes 2097152 | tf_op jit(solution)/shard_map/pallas_call | solution.py:89
  (274 shorter events, 108.4 us)
Async XLA Ops:
  2.6 48.7 %collective-permute-start.12 = (bf16[2,128,1024]{2,1,0:T(8,128)(2,1)}, bf16[2,128,1024]{2,1,0:T(8,128)(2,1)}, u32[]{:S(2)}, u32[]{:S(2)}) collective-permute-start(bf16[2,128,1024]{2,1,0:T(8,128)(2,1)} %pad_maximum_fusion.36), channel_id=1, source_target_pairs={{0,1},{1,2},{2,3},{3,0},{4,5},{5,6},{6,7},{7,4},{8,9},{9,10},{10,1... | collective-permute-start | bytes 1572872 | tf_op jit(solution)/shard_map/ppermute | solution.py:133
  5.6 48.2 %collective-permute-start.13 = (bf16[2,128,1024]{2,1,0:T(8,128)(2,1)}, bf16[2,128,1024]{2,1,0:T(8,128)(2,1)}, u32[]{:S(2)}, u32[]{:S(2)}) collective-permute-start(bf16[2,128,1024]{2,1,0:T(8,128)(2,1)} %pad_maximum_fusion.36), channel_id=1, source_target_pairs={{0,2},{1,3},{2,0},{3,1},{4,6},{5,7},{6,4},{7,5},{8,10},{9,11},{10,... | collective-permute-start | bytes 1572872 | tf_op jit(solution)/shard_map/ppermute | solution.py:133
  8.2 47.3 %collective-permute-start.14 = (bf16[2,128,1024]{2,1,0:T(8,128)(2,1)}, bf16[2,128,1024]{2,1,0:T(8,128)(2,1)}, u32[]{:S(2)}, u32[]{:S(2)}) collective-permute-start(bf16[2,128,1024]{2,1,0:T(8,128)(2,1)} %pad_maximum_fusion.36), channel_id=1, source_target_pairs={{0,3},{1,0},{2,1},{3,2},{4,7},{5,4},{6,5},{7,6},{8,11},{9,8},{10,9... | collective-permute-start | bytes 1572872 | tf_op jit(solution)/shard_map/ppermute | solution.py:133
  31.6 11.4 %collective-permute-start.9 = (bf16[3,64,1024]{2,1,0:T(8,128)(2,1)}, bf16[3,64,1024]{2,1,0:T(8,128)(2,1)}, u32[]{:S(2)}, u32[]{:S(2)}) collective-permute-start(bf16[3,64,1024]{2,1,0:T(8,128)(2,1)} %slice.465), channel_id=1, source_target_pairs={{0,4},{4,0},{8,12},{12,8},{1,5},{5,1},{9,13},{13,9},{2,6},{6,2},{1... | collective-permute-start | bytes 1179656 | tf_op jit(solution)/shard_map/ppermute | solution.py:162
  34.4 10.8 %collective-permute-start.6 = (bf16[3,64,1024]{2,1,0:T(8,128)(2,1)}, bf16[3,64,1024]{2,1,0:T(8,128)(2,1)}, u32[]{:S(2)}, u32[]{:S(2)}) collective-permute-start(bf16[3,64,1024]{2,1,0:T(8,128)(2,1)} %slice.459), channel_id=1, source_target_pairs={{0,4},{4,0},{8,12},{12,8},{1,5},{5,1},{9,13},{13,9},{2,6},{6,2},{1... | collective-permute-start | bytes 1179656 | tf_op jit(solution)/shard_map/ppermute | solution.py:162
  47.5 39.8 %collective-permute-start.10 = (bf16[3,64,1024]{2,1,0:T(8,128)(2,1)}, bf16[3,64,1024]{2,1,0:T(8,128)(2,1)}, u32[]{:S(2)}, u32[]{:S(2)}) collective-permute-start(bf16[3,64,1024]{2,1,0:T(8,128)(2,1)} %add_convert_fusion.5), channel_id=1, source_target_pairs={{0,8},{4,12},{8,0},{12,4},{1,9},{5,13},{9,1},{13,5},{2,10},{6,14},... | collective-permute-start | bytes 1179656 | tf_op jit(solution)/shard_map/ppermute | solution.py:121
  49.9 39.2 %collective-permute-start.7 = (bf16[3,64,1024]{2,1,0:T(8,128)(2,1)}, bf16[3,64,1024]{2,1,0:T(8,128)(2,1)}, u32[]{:S(2)}, u32[]{:S(2)}) collective-permute-start(bf16[3,64,1024]{2,1,0:T(8,128)(2,1)} %add_convert_fusion.6), channel_id=1, source_target_pairs={{0,8},{4,12},{8,0},{12,4},{1,9},{5,13},{9,1},{13,5},{2,10},{6,14},... | collective-permute-start | bytes 1179656 | tf_op jit(solution)/shard_map/ppermute | solution.py:121
  51.3 39.5 %collective-permute-start.4 = (bf16[3,64,1024]{2,1,0:T(8,128)(2,1)}, bf16[3,64,1024]{2,1,0:T(8,128)(2,1)}, u32[]{:S(2)}, u32[]{:S(2)}) collective-permute-start(bf16[3,64,1024]{2,1,0:T(8,128)(2,1)} %add_convert_fusion.7), channel_id=1, source_target_pairs={{0,8},{4,12},{8,0},{12,4},{1,9},{5,13},{9,1},{13,5},{2,10},{6,14},... | collective-permute-start | bytes 1179656 | tf_op jit(solution)/shard_map/ppermute | solution.py:121
  53.9 39.0 %collective-permute-start.1 = (bf16[3,64,1024]{2,1,0:T(8,128)(2,1)}, bf16[3,64,1024]{2,1,0:T(8,128)(2,1)}, u32[]{:S(2)}, u32[]{:S(2)}) collective-permute-start(bf16[3,64,1024]{2,1,0:T(8,128)(2,1)} %add_convert_fusion.8), channel_id=1, source_target_pairs={{0,8},{4,12},{8,0},{12,4},{1,9},{5,13},{9,1},{13,5},{2,10},{6,14},... | collective-permute-start | bytes 1179656 | tf_op jit(solution)/shard_map/ppermute | solution.py:121
  79.7 22.6 %collective-permute-start.24 = (bf16[3,192,1024]{2,1,0:T(8,128)(2,1)}, bf16[3,192,1024]{2,1,0:T(8,128)(2,1)}, u32[]{:S(2)}, u32[]{:S(2)}) collective-permute-start(bf16[3,192,1024]{2,1,0:T(8,128)(2,1)} %slice.487), channel_id=1, source_target_pairs={{0,4},{4,0},{8,12},{12,8},{1,5},{5,1},{9,13},{13,9},{2,6},{6,2},{1... | collective-permute-start | bytes 3538952 | tf_op jit(solution)/shard_map/ppermute | solution.py:162
  87.3 19.8 %collective-permute-start.21 = (bf16[3,192,1024]{2,1,0:T(8,128)(2,1)}, bf16[3,192,1024]{2,1,0:T(8,128)(2,1)S(1)}, u32[]{:S(2)}, u32[]{:S(2)}) collective-permute-start(bf16[3,192,1024]{2,1,0:T(8,128)(2,1)} %slice.482), channel_id=1, source_target_pairs={{0,4},{4,0},{8,12},{12,8},{1,5},{5,1},{9,13},{13,9},{2,6},{6,2},{1... | collective-permute-start | bytes 3538952 | tf_op jit(solution)/shard_map/ppermute | solution.py:162
  89.2 19.3 %collective-permute-start.18 = (bf16[3,192,1024]{2,1,0:T(8,128)(2,1)}, bf16[3,192,1024]{2,1,0:T(8,128)(2,1)S(1)}, u32[]{:S(2)}, u32[]{:S(2)}) collective-permute-start(bf16[3,192,1024]{2,1,0:T(8,128)(2,1)} %slice.477), channel_id=1, source_target_pairs={{0,4},{4,0},{8,12},{12,8},{1,5},{5,1},{9,13},{13,9},{2,6},{6,2},{1... | collective-permute-start | bytes 3538952 | tf_op jit(solution)/shard_map/ppermute | solution.py:162
  90.9 19.5 %collective-permute-start.15 = (bf16[3,192,1024]{2,1,0:T(8,128)(2,1)S(1)}, bf16[3,192,1024]{2,1,0:T(8,128)(2,1)S(1)}, u32[]{:S(2)}, u32[]{:S(2)}) collective-permute-start(bf16[3,192,1024]{2,1,0:T(8,128)(2,1)S(1)} %copy-done.45), channel_id=1, source_target_pairs={{0,4},{4,0},{8,12},{12,8},{1,5},{5,1},{9,13},{13,9},{2,6},{6,2},{1... | collective-permute-start | bytes 3538952 | tf_op jit(solution)/shard_map/ppermute | solution.py:162
  99.7 6.7 %collective-permute-start.2 = (bf16[3,64,1024]{2,1,0:T(8,128)(2,1)S(1)}, bf16[3,64,1024]{2,1,0:T(8,128)(2,1)S(1)}, u32[]{:S(2)}, u32[]{:S(2)}) collective-permute-start(bf16[3,64,1024]{2,1,0:T(8,128)(2,1)S(1)} %pad_maximum_fusion.37), channel_id=1, source_target_pairs={{0,4},{4,0},{8,12},{12,8},{1,5},{5,1},{9,13},{13,9},{2,6},{6,2},{1... | collective-permute-start | bytes 1179656 | tf_op jit(solution)/shard_map/ppermute | solution.py:165
  104.8 28.8 %collective-permute-start.25 = (bf16[3,192,1024]{2,1,0:T(8,128)(2,1)S(1)}, bf16[3,192,1024]{2,1,0:T(8,128)(2,1)S(1)}, u32[]{:S(2)}, u32[]{:S(2)}) collective-permute-start(bf16[3,192,1024]{2,1,0:T(8,128)(2,1)S(1)} %add_convert_fusion), channel_id=1, source_target_pairs={{0,8},{4,12},{8,0},{12,4},{1,9},{5,13},{9,1},{13,5},{2,10},{6,14},... | collective-permute-start | bytes 3538952 | tf_op jit(solution)/shard_map/ppermute | solution.py:121
  107.7 51.2 %collective-permute-start.22 = (bf16[3,192,1024]{2,1,0:T(8,128)(2,1)S(1)}, bf16[3,192,1024]{2,1,0:T(8,128)(2,1)S(1)}, u32[]{:S(2)}, u32[]{:S(2)}) collective-permute-start(bf16[3,192,1024]{2,1,0:T(8,128)(2,1)S(1)} %add_convert_fusion.1), channel_id=1, source_target_pairs={{0,8},{4,12},{8,0},{12,4},{1,9},{5,13},{9,1},{13,5},{2,10},{6,14},... | collective-permute-start | bytes 3538952 | tf_op jit(solution)/shard_map/ppermute | solution.py:121
  109.3 74.9 %collective-permute-start.19 = (bf16[3,192,1024]{2,1,0:T(8,128)(2,1)S(1)}, bf16[3,192,1024]{2,1,0:T(8,128)(2,1)S(1)}, u32[]{:S(2)}, u32[]{:S(2)}) collective-permute-start(bf16[3,192,1024]{2,1,0:T(8,128)(2,1)S(1)} %add_convert_fusion.2), channel_id=1, source_target_pairs={{0,8},{4,12},{8,0},{12,4},{1,9},{5,13},{9,1},{13,5},{2,10},{6,14},... | collective-permute-start | bytes 3538952 | tf_op jit(solution)/shard_map/ppermute | solution.py:121
  110.8 98.2 %collective-permute-start.16 = (bf16[3,192,1024]{2,1,0:T(8,128)(2,1)S(1)}, bf16[3,192,1024]{2,1,0:T(8,128)(2,1)S(1)}, u32[]{:S(2)}, u32[]{:S(2)}) collective-permute-start(bf16[3,192,1024]{2,1,0:T(8,128)(2,1)S(1)} %add_convert_fusion.3), channel_id=1, source_target_pairs={{0,8},{4,12},{8,0},{12,4},{1,9},{5,13},{9,1},{13,5},{2,10},{6,14},... | collective-permute-start | bytes 3538952 | tf_op jit(solution)/shard_map/ppermute | solution.py:121
  134.8 84.3 %collective-permute-start.26 = (bf16[3,192,1024]{2,1,0:T(8,128)(2,1)S(1)}, bf16[3,192,1024]{2,1,0:T(8,128)(2,1)S(1)}, u32[]{:S(2)}, u32[]{:S(2)}) collective-permute-start(bf16[3,192,1024]{2,1,0:T(8,128)(2,1)S(1)} %pad_maximum_fusion.11), channel_id=1, source_target_pairs={{0,4},{4,0},{8,12},{12,8},{1,5},{5,1},{9,13},{13,9},{2,6},{6,2},{1... | collective-permute-start | bytes 3538952 | tf_op jit(solution)/shard_map/ppermute | solution.py:165
  160.1 50.3 %collective-permute-start.23 = (bf16[3,192,1024]{2,1,0:T(8,128)(2,1)S(1)}, bf16[3,192,1024]{2,1,0:T(8,128)(2,1)S(1)}, u32[]{:S(2)}, u32[]{:S(2)}) collective-permute-start(bf16[3,192,1024]{2,1,0:T(8,128)(2,1)S(1)} %pad_maximum_fusion.10), channel_id=1, source_target_pairs={{0,4},{4,0},{8,12},{12,8},{1,5},{5,1},{9,13},{13,9},{2,6},{6,2},{1... | collective-permute-start | bytes 3538952 | tf_op jit(solution)/shard_map/ppermute | solution.py:165
  185.4 27.1 %collective-permute-start.20 = (bf16[3,192,1024]{2,1,0:T(8,128)(2,1)S(1)}, bf16[3,192,1024]{2,1,0:T(8,128)(2,1)S(1)}, u32[]{:S(2)}, u32[]{:S(2)}) collective-permute-start(bf16[3,192,1024]{2,1,0:T(8,128)(2,1)S(1)} %pad_maximum_fusion.9), channel_id=1, source_target_pairs={{0,4},{4,0},{8,12},{12,8},{1,5},{5,1},{9,13},{13,9},{2,6},{6,2},{1... | collective-permute-start | bytes 3538952 | tf_op jit(solution)/shard_map/ppermute | solution.py:165
  221.6 46.0 %collective-permute-start.29 = (bf16[128,1024]{1,0:T(8,128)(2,1)S(1)}, bf16[128,1024]{1,0:T(8,128)(2,1)S(1)}, u32[]{:S(2)}, u32[]{:S(2)}) collective-permute-start(bf16[128,1024]{1,0:T(8,128)(2,1)S(1)} %pad_maximum_fusion.64), channel_id=1, source_target_pairs={{0,1},{1,2},{2,3},{3,0},{4,5},{5,6},{6,7},{7,4},{8,9},{9,10},{10,1... | collective-permute-start | bytes 786440 | tf_op jit(solution)/shard_map/ppermute | solution.py:192
  222.4 45.3 %collective-permute-start.28 = (bf16[128,1024]{1,0:T(8,128)(2,1)S(1)}, bf16[128,1024]{1,0:T(8,128)(2,1)S(1)}, u32[]{:S(2)}, u32[]{:S(2)}) collective-permute-start(bf16[128,1024]{1,0:T(8,128)(2,1)S(1)} %pad_maximum_fusion.63), channel_id=1, source_target_pairs={{0,2},{1,3},{2,0},{3,1},{4,6},{5,7},{6,4},{7,5},{8,10},{9,11},{10,... | collective-permute-start | bytes 786440 | tf_op jit(solution)/shard_map/ppermute | solution.py:192
  224.6 43.1 %collective-permute-start.27 = (bf16[128,1024]{1,0:T(8,128)(2,1)S(1)}, bf16[128,1024]{1,0:T(8,128)(2,1)S(1)}, u32[]{:S(2)}, u32[]{:S(2)}) collective-permute-start(bf16[128,1024]{1,0:T(8,128)(2,1)S(1)} %pad_maximum_fusion.62), channel_id=1, source_target_pairs={{0,3},{1,0},{2,1},{3,2},{4,7},{5,4},{6,5},{7,6},{8,11},{9,8},{10,9... | collective-permute-start | bytes 786440 | tf_op jit(solution)/shard_map/ppermute | solution.py:192
  (56 other events, 304.9 us)

commit v2 on v0

v2 whole, which is shorter than its diff:
```python
import functools

import jax
import jax.numpy as jnp
from jax import lax
from jax.experimental import pallas as pl
from jax.experimental.pallas import tpu as pltpu
from jax.sharding import PartitionSpec as P

BLK = 128
STEP = 256
CONTRACT_ROWS = (((0,), (0,)), ((), ()))
CONTRACT_COLUMNS = (((1,), (1,)), ((), ()))
PARAMS = pltpu.CompilerParams(vmem_limit_bytes=40 * 2**20)


def masked(weight, lines):
    rows, columns = weight.shape
    blocked = weight.reshape(rows // BLK, BLK, columns) * lines
    return blocked.reshape(rows, columns)


def ahead(left, weight):
    return jnp.dot(left, weight, preferred_element_type=jnp.float32)


def behind(left, weight):
    return lax.dot_general(left, weight, CONTRACT_COLUMNS, preferred_element_type=jnp.float32)


def outer(left, right):
    return lax.dot_general(left, right, CONTRACT_ROWS, preferred_element_type=jnp.float32)


def cost(flops, moved):
    return pl.CostEstimate(flops=flops, bytes_accessed=moved, transcendentals=0)


ANY = pl.BlockSpec(memory_space=pl.ANY)


def product_kernel(x_ref, g_ref, u_ref, d_ref, gl_ref, dl_ref, *refs):
    mine_ref, theirs_ref = refs[-2:]
    half = mine_ref.shape[1]
    tokens, cotangent = x_ref[0], x_ref[1]

    def put(i, value):
        value = value.astype(jnp.bfloat16)
        mine_ref[i] = value[:half]
        theirs_ref[i] = value[half:]

    put(0, ahead(tokens, masked(g_ref[...], gl_ref[...])))
    put(1, ahead(tokens, masked(u_ref[...], gl_ref[...])))
    put(2, behind(cotangent, masked(d_ref[...], dl_ref[...])))


def products(x, weights, lines, k, size, after):
    gate, up, down = weights
    count, height = x.shape[1:]
    step = min(STEP, size)
    base = k * size // step
    out = jax.ShapeDtypeStruct((3, count // 2, size), jnp.bfloat16)
    columns = pl.BlockSpec((height, step), lambda j: (0, base + j))
    return pl.pallas_call(
        product_kernel,
        out_shape=(out, out),
        grid=(size // step,),
        in_specs=[
            pl.BlockSpec((2, count, height), lambda j: (0, 0, 0)),
            columns,
            columns,
            pl.BlockSpec((step, height), lambda j: (base + j, 0)),
            pl.BlockSpec((height // BLK, 1, step), lambda j: (0, 0, base + j)),
            pl.BlockSpec((step // BLK, 1, height), lambda j: (base + j, 0, 0)),
        ]
        + [ANY] * len(after),
        out_specs=[pl.BlockSpec((3, count // 2, step), lambda j: (0, 0, j))] * 2,
        compiler_params=PARAMS,
        cost_estimate=cost(6 * count * height * size, 6 * height * size),
    )(x, gate, up, down, *lines, *after)


def delta_kernel(n, *refs):
    out_ref = refs[-1]
    gate, up, hidden_delta = (
        functools.reduce(lambda a, b: a + b, [r[i].astype(jnp.float32) for r in refs[:n]]) for i in range(3)
    )
    sigma = jax.nn.sigmoid(gate)
    active = gate * sigma
    out_ref[0] = (active * up).astype(jnp.bfloat16)
    out_ref[1] = (hidden_delta * up * sigma * (1.0 + gate * (1.0 - sigma))).astype(jnp.bfloat16)
    out_ref[2] = (hidden_delta * active).astype(jnp.bfloat16)


def deltas(parts, after):
    three, count, size = parts[0].shape
    step = min(STEP, size)
    spec = pl.BlockSpec((three, count, step), lambda j: (0, 0, j))
    return pl.pallas_call(
        functools.partial(delta_kernel, len(parts)),
        out_shape=jax.ShapeDtypeStruct(parts[0].shape, jnp.bfloat16),
        grid=(size // step,),
        in_specs=[spec] * len(parts) + [ANY] * len(after),
        out_specs=spec,
        compiler_params=PARAMS,
        cost_estimate=cost(60 * count * size, 18 * count * size),
    )(*parts, *after)


def term_kernel(first, *refs):
    gd_mine, gd_theirs, ud_mine, ud_theirs, g_ref, u_ref, l_ref = refs[:7]
    out_ref = refs[-1]
    gate_delta = jnp.concatenate([gd_mine[0], gd_theirs[0]], axis=0)
    up_delta = jnp.concatenate([ud_mine[0], ud_theirs[0]], axis=0)
    value = behind(gate_delta, masked(g_ref[...], l_ref[...])) + behind(up_delta, masked(u_ref[...], l_ref[...]))
    out_ref[...] = value if first else refs[7][...] + value


def add_term(pair, weights, lines, k, size, term):
    gate, up, _ = weights
    height = gate.shape[0]
    count = 2 * pair[0].shape[1]
    step = min(STEP, height)
    held = pl.BlockSpec((count, step), lambda j: (0, j))
    rows = pl.BlockSpec((step, size), lambda j: (j, k))
    pieces = [pl.BlockSpec((1, count // 2, size), lambda j, i=i: (i, 0, 0)) for i in (1, 1, 2, 2)]
    extra = [] if term is None else [term]
    return pl.pallas_call(
        functools.partial(term_kernel, term is None),
        out_shape=jax.ShapeDtypeStruct((count, height), jnp.float32),
        grid=(height // step,),
        in_specs=pieces
        + [rows, rows, pl.BlockSpec((step // BLK, 1, size), lambda j: (j, 0, k))]
        + [held] * len(extra),
        out_specs=held,
        compiler_params=PARAMS,
        cost_estimate=cost(4 * count * height * size, 4 * height * size),
    )(pair[0], pair[1], pair[0], pair[1], gate, up, lines[0], *extra)


def gradient_kernel(n, *refs):
    parts = refs[:n]
    tokens_ref, cotangent_ref, gl_ref, dl_ref = refs[n : n + 4]
    gate_ref, up_ref, down_ref = refs[-3:]

    def put(ref, product, lines):
        rows, columns = product.shape
        blocked = product.reshape(rows // BLK, BLK, columns) * lines.astype(jnp.float32)
        ref[...] = blocked.reshape(rows, columns).astype(jnp.bfloat16)

    hidden, gate_delta, up_delta = (jnp.concatenate([p[i] for p in parts], axis=0) for i in range(3))
    put(gate_ref, ahead(tokens_ref[...], gate_delta), gl_ref[...])
    put(up_ref, ahead(tokens_ref[...], up_delta), gl_ref[...])
    put(down_ref, outer(hidden, cotangent_ref[...]), dl_ref[...])


def gradients(parts, tokens_t, cotangent, lines, k, size, width, into):
    height, depth = tokens_t.shape
    step = min(STEP, size)
    base = k * size // step
    n = len(parts)
    columns = pl.BlockSpec((height, step), lambda j: (0, base + j))
    down_rows = pl.BlockSpec((step, height), lambda j: (base + j, 0))
    wide = jax.ShapeDtypeStruct((height, width), jnp.bfloat16)
    return pl.pallas_call(
        functools.partial(gradient_kernel, n),
        out_shape=(wide, wide, jax.ShapeDtypeStruct((width, height), jnp.bfloat16)),
        grid=(size // step,),
        in_specs=[pl.BlockSpec((3, p.shape[1], step), lambda j: (0, 0, j)) for p in parts]
        + [
            pl.BlockSpec((height, depth), lambda j: (0, 0)),
            pl.BlockSpec((depth, height), lambda j: (0, 0)),
            pl.BlockSpec((height // BLK, 1, step), lambda j: (0, 0, base + j)),
            pl.BlockSpec((step // BLK, 1, height), lambda j: (base + j, 0, 0)),
        ]
        + [ANY] * len(into),
        out_specs=(columns, columns, down_rows),
        input_output_aliases={n + 4 + i: i for i in range(len(into))},
        compiler_params=PARAMS,
        cost_estimate=cost(6 * height * depth * size, 6 * height * size),
    )(*parts, tokens_t, cotangent, *lines, *into)


def on_device(n_row, n_col, tokens, cotangent, gate_weight, up_weight, down_weight, gate_keep, down_keep):
    core = lax.rem(lax.axis_index("row"), 2)
    chips = n_row // 2
    swap = [(i, i ^ 1) for i in range(n_row)]
    height, width = gate_weight.shape
    own_rows = tokens.shape[0]
    half = own_rows // 2
    size = min(1024, width)
    chunks = width // size
    weights = (gate_weight, up_weight, down_weight)
    lines = tuple(jnp.repeat(keep, BLK, axis=1).astype(jnp.bfloat16)[:, None, :] for keep in (gate_keep, down_keep))

    def core_order(value):
        return jnp.where(core == 0, value, jnp.concatenate([value[:, half:], value[:, :half]], axis=1))

    def shifted(value, s):
        return lax.ppermute(value, "col", [(i, (i + s) % n_col) for i in range(n_col)])

    both = core_order(jnp.stack([tokens, cotangent]))
    block = {0: both}
    for s in range(1, n_col // 2 + 1):
        block[s] = shifted(block[s - 1], 1)
        if n_col - s > n_col // 2:
            block[n_col - s] = shifted(block[(n_col - s + 1) % n_col], -1)
    near = [s for s in dict.fromkeys((1, n_col - 1)) if 0 < s < n_col]
    far = [s for s in range(2, n_col - 1)]
    shifts = [g for g in ([0], near, far) if g]
    groups = [
        jnp.concatenate([block[s][:, :half] for s in g] + [block[s][:, half:] for s in g], axis=1) for g in shifts
    ]
    rows = jnp.concatenate(groups, axis=1)
    tokens_t = rows[0].T

    order = [(0, k) for k in range(chunks)]
    if len(groups) > 1:
        order += [(1, 0)] + [(1, 1)] * (chunks > 1)
    if len(groups) > 2:
        for k in range(chunks):
            order += [(2, k)] + [(1, k + 2)] * (k + 2 < chunks)
    elif len(groups) > 1:
        order += [(1, k) for k in range(2, chunks)]

    mine_of, pairs, terms = [], {}, [None] * len(groups)
    seen, into, ready = [0] * chunks, (), {}
    for at, (g, k) in enumerate(order):
        after = [mine_of[at - 2]] if at >= 2 else []
        mine, theirs = products(groups[g], weights, lines, k, size, after)
        came = lax.ppermute(theirs, "row", swap)
        mine = (mine.astype(jnp.float32) + came.astype(jnp.float32)).astype(jnp.bfloat16)
        mine_of.append(mine)
        parts = [mine]
        for c in range(1, chips):
            parts.append(lax.ppermute(mine, "row", [(i, (i + 2 * c) % n_row) for i in range(n_row)]))
        result = deltas(parts, ready.get(at, []))
        pairs[g, k] = (result, lax.ppermute(result, "row", swap))
        terms[g] = add_term(pairs[g, k], weights, lines, k, size, terms[g])
        done = [terms[g]]
        seen[k] += 1
        if seen[k] == len(groups):
            pieces = [p for gg in range(len(groups)) for p in pairs[gg, k]]
            into = gradients(pieces, tokens_t, rows[1], lines, k, size, width, into)
            done += list(into)
        ready[at + 2] = done

    total = terms[0]
    for g in range(1, len(groups)):
        sent = terms[g].astype(jnp.bfloat16)
        middle = half * len(shifts[g])
        for at, s in enumerate(shifts[g]):
            low = at * half
            piece = jnp.concatenate([sent[low : low + half], sent[middle + low : middle + low + half]], axis=0)
            total = total + shifted(piece, -s).astype(jnp.float32)
    return (core_order(total[None])[0].astype(jnp.bfloat16), *into)


def solution(mesh):
    placed = (
        P(("groups", "col"), "row"),
        P(("groups", "col"), "row"),
        P("row", "col"),
        P("row", "col"),
        P("col", "row"),
        P("row", "col"),
        P("col", "row"),
    )
    return jax.shard_map(
        functools.partial(on_device, mesh.shape["row"], mesh.shape["col"]),
        mesh=mesh,
        in_specs=placed,
        out_specs=(
            P(("groups", "col"), "row"),
            P(("groups", "row"), "col"),
            P(("groups", "row"), "col"),
            P(("groups", "col"), "row"),
        ),
        check_vma=False,
    )
```

time: 385 us -> 258 us (0.67)
  Pallas kernels: 0 us -> 142 us
  waiting for transfers between devices: 172 us -> 53.9 us
  matrix products: 78.6 us -> 0 us
  local copies, waits for them, and re-layouts: 80.2 us -> 16.3 us
  starting transfers between devices: 0.27 us -> 28.9 us
  other arithmetic: 38.1 us -> 12.8 us
  between operations: 14.2 us -> 1.77 us
    pallas_call x0 -> x40, Pallas kernels: none -> 142 us  [the longest x12 54.9 us: products(): pl.pallas_call(product_kernel, out_shape=(out, out), grid=(size // step,)...]
    unnamed x8 -> x0, waiting for transfers between devices: 101 us -> none
    dot_general x8 -> x0, matrix products: 78.6 us -> none  [the longest x3 31 us: dense_behind(): lax.dot_general(left, weight, CONTRACT_COLUMNS, preferred_element_type=jn...]
    all_gather x5 -> x0, waiting for transfers between devices: 68.6 us -> none  [the longest x1 34 us: on_device(): lax.all_gather(gate_delta, 'row', axis=0, tiled=True)]
    unnamed x21 -> x100, local copies, waits for them, and re-layouts: 68.1 us -> 13.2 us
    ppermute x0 -> x42, waiting for transfers between devices: none -> 53.9 us  [the longest x12 29.3 us: on_device(): lax.ppermute(mine, 'row', [(i, (i + 2 * c) % n_row) for i in range(n_row)])]
    ppermute x0 -> x42, starting transfers between devices: none -> 28.9 us  [the longest x12 13.7 us: on_device(): lax.ppermute(mine, 'row', [(i, (i + 2 * c) % n_row) for i in range(n_row)])]
    concatenate x1 -> x3, other arithmetic: 22 us -> 0.11 us  [the longest x1 0.07 us: on_device(): jnp.concatenate([block[s][:, :half] for s in g] + [block[s][:, half:] for...]
  transfers between devices with their start and end apart: 7 -> 42, of which waited for: 5 -> 8; matrix products, arithmetic and copies ran while one was open for 33% -> 4% of each run, Pallas kernels for 0% -> 54%
where the time goes in v2:
time: 258 us; the launch traced here: 256 us
  Pallas kernels  142 us (55%)
  waiting for transfers between devices  53.9 us (21%)
  starting transfers between devices  28.9 us (11%)
  local copies, waits for them, and re-layouts  16.3 us (6%)
  other arithmetic  12.8 us (5%)
    pallas_call x12, Pallas kernels, products(): pl.pallas_call(product_kernel, out_shape=(out, out), grid=(size // step,)...  54.9 us
    pallas_call x12, Pallas kernels, add_term(): pl.pallas_call(functools.partial(term_kernel, term is None), out_shape=ja...  47 us
    ppermute x12, waiting for transfers between devices, on_device(): lax.ppermute(mine, 'row', [(i, (i + 2 * c) % n_row) for i in range(n_row)])  29.3 us
    pallas_call x4, Pallas kernels, gradients(): pl.pallas_call(functools.partial(gradient_kernel, n), out_shape=(wide, wi...  24.6 us
    ppermute x6, waiting for transfers between devices, shifted(): lax.ppermute(value, 'col', [(i, (i + s) % n_col) for i in range(n_col)])  24.5 us
    pallas_call x12, Pallas kernels, deltas(): pl.pallas_call(functools.partial(delta_kernel, len(parts)), out_shape=jax...  15.8 us
    ppermute x12, starting transfers between devices, on_device(): lax.ppermute(mine, 'row', [(i, (i + 2 * c) % n_row) for i in range(n_row)])  13.7 us
    unnamed x100, local copies, waits for them, and re-layouts  13.2 us
  transfers between devices with their start and end apart: 42, of which 8 were waited for; matrix products, arithmetic and copies ran while one was open for 4% of the time, Pallas kernels for 54%

profile of v2, /device:TPU:0, one launch (start us, length us, event | category | flops | bytes accessed | tf_op | source)
XLA Modules:
  0.0 255.8 jit_solution(16310195450330374869)
XLA Ops:
  8.2 4.3 %shard_map.105 = (bf16[3,64,1024]{2,1,0:T(8,128)(2,1)S(1)}, bf16[3,64,1024]{2,1,0:T(8,128)(2,1)S(1)}) custom-call(bf16[2,128,1024]{2,1,0:T(8,128)(2,1)S(1)} %get-tuple-element.77.x_ref, bf16[1024,4096]{1,0:T(8,128)(2,1)S(1)} %copy-done, bf16[1024,4096]{1,0:T(8,128)(2,1)} %refs_5_.23, bf16[4096,1024]{1,0:T(8,128)(2,1)} %d_ref.23, ...), custom_call_target="tpu_custom_call" | custom-call | flops 805306368 | bytes 6291456 | tf_op jit(solution)/shard_map/pallas_call | solution.py:64
  13.0 4.3 %shard_map.102 = (bf16[3,64,1024]{2,1,0:T(8,128)(2,1)S(1)}, bf16[3,64,1024]{2,1,0:T(8,128)(2,1)S(1)}) custom-call(bf16[2,128,1024]{2,1,0:T(8,128)(2,1)S(1)} %get-tuple-element.77.x_ref, bf16[1024,4096]{1,0:T(8,128)(2,1)S(1)} %copy-done, bf16[1024,4096]{1,0:T(8,128)(2,1)} %refs_5_.23, bf16[4096,1024]{1,0:T(8,128)(2,1)} %d_ref.23, ...), custom_call_target="tpu_custom_call" | custom-call | flops 805306368 | bytes 6291456 | tf_op jit(solution)/shard_map/pallas_call | solution.py:64
  24.4 4.3 %shard_map.110 = (bf16[3,64,1024]{2,1,0:T(8,128)(2,1)S(1)}, bf16[3,64,1024]{2,1,0:T(8,128)(2,1)S(1)}) custom-call(bf16[2,128,1024]{2,1,0:T(8,128)(2,1)S(1)} %get-tuple-element.77.x_ref, bf16[1024,4096]{1,0:T(8,128)(2,1)S(1)} %copy-done, bf16[1024,4096]{1,0:T(8,128)(2,1)} %refs_5_.23, bf16[4096,1024]{1,0:T(8,128)(2,1)} %d_ref.23, ...), custom_call_target="tpu_custom_call" | custom-call | flops 805306368 | bytes 6291456 | tf_op jit(solution)/shard_map/pallas_call | solution.py:64
  29.4 4.8 %shard_map.103 = (bf16[3,64,1024]{2,1,0:T(8,128)(2,1)S(1)}, bf16[3,64,1024]{2,1,0:T(8,128)(2,1)S(1)}) custom-call(bf16[2,128,1024]{2,1,0:T(8,128)(2,1)S(1)} %get-tuple-element.77.x_ref, bf16[1024,4096]{1,0:T(8,128)(2,1)S(1)} %copy-done, bf16[1024,4096]{1,0:T(8,128)(2,1)} %refs_5_.23, bf16[4096,1024]{1,0:T(8,128)(2,1)} %d_ref.23, ...), custom_call_target="tpu_custom_call" | custom-call | flops 805306368 | bytes 6291456 | tf_op jit(solution)/shard_map/pallas_call | solution.py:64
  35.3 10.0 %collective-permute-done.13 = bf16[2,128,1024]{2,1,0:T(8,128)(2,1)S(1)} collective-permute-done((bf16[2,128,1024]{2,1,0:T(8,128)(2,1)S(1)}, bf16[2,128,1024]{2,1,0:T(8,128)(2,1)S(1)}, u32[]{:S(2)}, u32[]{:S(2)}) %collective-permute-start.13) | collective-permute-done | bytes 524320 | tf_op jit(solution)/shard_map/ppermute | solution.py:200
  46.8 4.6 %shard_map.118 = (bf16[3,128,1024]{2,1,0:T(8,128)(2,1)S(1)}, bf16[3,128,1024]{2,1,0:T(8,128)(2,1)S(1)}) custom-call(bf16[2,256,1024]{2,1,0:T(8,128)(2,1)S(1)} %pad_maximum_fusion.x_ref, bf16[1024,4096]{1,0:T(8,128)(2,1)S(1)} %bitcast.15, bf16[1024,4096]{1,0:T(8,128)(2,1)} %refs_5_.23, bf16[4096,1024]{1,0:T(8,128)(2,1)} %d_ref.23, ...), custom_call_target="tpu_custom_call" | custom-call | flops 1610612736 | bytes 6291456 | tf_op jit(solution)/shard_map/pallas_call | solution.py:64
  52.7 4.7 %shard_map.114 = (bf16[3,128,1024]{2,1,0:T(8,128)(2,1)S(1)}, bf16[3,128,1024]{2,1,0:T(8,128)(2,1)S(1)}) custom-call(bf16[2,256,1024]{2,1,0:T(8,128)(2,1)S(1)} %pad_maximum_fusion.x_ref, bf16[1024,4096]{1,0:T(8,128)(2,1)S(1)} %bitcast.15, bf16[1024,4096]{1,0:T(8,128)(2,1)} %refs_5_.23, bf16[4096,1024]{1,0:T(8,128)(2,1)} %d_ref.23, ...), custom_call_target="tpu_custom_call" | custom-call | flops 1610612736 | bytes 6291456 | tf_op jit(solution)/shard_map/pallas_call | solution.py:64
  64.0 5.4 %collective-permute-done.10.refs_1_ = bf16[3,64,1024]{2,1,0:T(8,128)(2,1)S(1)} collective-permute-done((bf16[3,64,1024]{2,1,0:T(8,128)(2,1)S(1)}, bf16[3,64,1024]{2,1,0:T(8,128)(2,1)S(1)}, u32[]{:S(2)}, u32[]{:S(2)}) %collective-permute-start.10) | collective-permute-done | bytes 393248 | tf_op jit(solution)/shard_map/ppermute | solution.py:236
  80.7 4.7 %shard_map.115 = (bf16[3,128,1024]{2,1,0:T(8,128)(2,1)S(1)}, bf16[3,128,1024]{2,1,0:T(8,128)(2,1)S(1)}) custom-call(bf16[2,256,1024]{2,1,0:T(8,128)(2,1)S(1)} %pad_maximum_fusion.x_ref, bf16[1024,4096]{1,0:T(8,128)(2,1)S(1)} %bitcast.15, bf16[1024,4096]{1,0:T(8,128)(2,1)} %refs_5_.23, bf16[4096,1024]{1,0:T(8,128)(2,1)} %d_ref.23, ...), custom_call_target="tpu_custom_call" | custom-call | flops 1610612736 | bytes 6291456 | tf_op jit(solution)/shard_map/pallas_call | solution.py:64
  85.5 4.3 %shard_map.128 = (bf16[3,64,1024]{2,1,0:T(8,128)(2,1)S(1)}, bf16[3,64,1024]{2,1,0:T(8,128)(2,1)S(1)}) custom-call(bf16[2,128,1024]{2,1,0:T(8,128)(2,1)S(1)} %collective-permute-done.28.x_ref, bf16[1024,4096]{1,0:T(8,128)(2,1)S(1)} %bitcast.15, bf16[1024,4096]{1,0:T(8,128)(2,1)} %refs_5_.23, bf16[4096,1024]{1,0:T(8,128)(2,1)} %d_ref.23, ...), custom_call_target="tpu_custom_call" | custom-call | flops 805306368 | bytes 6291456 | tf_op jit(solution)/shard_map/pallas_call | solution.py:64
  98.3 4.3 %shard_map.129 = (bf16[3,64,1024]{2,1,0:T(8,128)(2,1)S(1)}, bf16[3,64,1024]{2,1,0:T(8,128)(2,1)S(1)}) custom-call(bf16[2,128,1024]{2,1,0:T(8,128)(2,1)S(1)} %collective-permute-done.28.x_ref, bf16[1024,4096]{1,0:T(8,128)(2,1)S(1)} %bitcast.15, bf16[1024,4096]{1,0:T(8,128)(2,1)} %refs_5_.23, bf16[4096,1024]{1,0:T(8,128)(2,1)} %d_ref.23, ...), custom_call_target="tpu_custom_call" | custom-call | flops 805306368 | bytes 6291456 | tf_op jit(solution)/shard_map/pallas_call | solution.py:64
  104.1 11.1 %collective-permute-done.19.refs_1_ = bf16[3,128,1024]{2,1,0:T(8,128)(2,1)S(1)} collective-permute-done((bf16[3,128,1024]{2,1,0:T(8,128)(2,1)S(1)}, bf16[3,128,1024]{2,1,0:T(8,128)(2,1)S(1)}, u32[]{:S(2)}, u32[]{:S(2)}) %collective-permute-start.19) | collective-permute-done | bytes 786464 | tf_op jit(solution)/shard_map/ppermute | solution.py:236
  117.9 4.7 %shard_map.116 = (bf16[3,128,1024]{2,1,0:T(8,128)(2,1)S(1)}, bf16[3,128,1024]{2,1,0:T(8,128)(2,1)S(1)}) custom-call(bf16[2,256,1024]{2,1,0:T(8,128)(2,1)S(1)} %pad_maximum_fusion.x_ref, bf16[1024,4096]{1,0:T(8,128)(2,1)S(1)} %bitcast.15, bf16[1024,4096]{1,0:T(8,128)(2,1)} %refs_5_.23, bf16[4096,1024]{1,0:T(8,128)(2,1)} %d_ref.23, ...), custom_call_target="tpu_custom_call" | custom-call | flops 1610612736 | bytes 6291456 | tf_op jit(solution)/shard_map/pallas_call | solution.py:64
  124.4 5.0 %shard_map.130 = (bf16[3,64,1024]{2,1,0:T(8,128)(2,1)S(1)}, bf16[3,64,1024]{2,1,0:T(8,128)(2,1)}) custom-call(bf16[2,128,1024]{2,1,0:T(8,128)(2,1)S(1)} %collective-permute-done.28.x_ref, bf16[1024,4096]{1,0:T(8,128)(2,1)S(1)} %bitcast.15, bf16[1024,4096]{1,0:T(8,128)(2,1)} %refs_5_.23, bf16[4096,1024]{1,0:T(8,128)(2,1)} %d_ref.23, ...), custom_call_target="tpu_custom_call" | custom-call | flops 805306368 | bytes 6291456 | tf_op jit(solution)/shard_map/pallas_call | solution.py:64
  134.7 10.5 %collective-permute-done.37.refs_1_ = bf16[3,64,1024]{2,1,0:T(8,128)(2,1)S(1)} collective-permute-done((bf16[3,64,1024]{2,1,0:T(8,128)(2,1)S(1)}, bf16[3,64,1024]{2,1,0:T(8,128)(2,1)S(1)}, u32[]{:S(2)}, u32[]{:S(2)}) %collective-permute-start.37) | collective-permute-done | bytes 393248 | tf_op jit(solution)/shard_map/ppermute | solution.py:236
  162.0 4.1 %shard_map.132.refs_2_.refs_7_ = f32[128,1024]{1,0:T(8,128)S(1)} custom-call(bf16[3,64,1024]{2,1,0:T(8,128)(2,1)} %shard_map.131.refs_0_.refs_2_.refs_4_, bf16[3,64,1024]{2,1,0:T(8,128)(2,1)} %collective-permute-done.38.refs_1_.refs_3_.refs_5_, bf16[3,64,1024]{2,1,0:T(8,128)(2,1)} %shard_map.131.refs_0_.refs_2_.refs_4_, ...), custom_call_target="tpu_custom_call" | custom-call | flops 536870912 | bytes 4194304 | tf_op jit(solution)/shard_map/pallas_call | solution.py:128
  166.2 6.2 %shard_map.133 = (bf16[1024,4096]{1,0:T(8,128)(2,1)}, bf16[1024,4096]{1,0:T(8,128)(2,1)}, bf16[4096,1024]{1,0:T(8,128)(2,1)}) custom-call(bf16[3,64,1024]{2,1,0:T(8,128)(2,1)S(1)} %copy-done.31, bf16[3,64,1024]{2,1,0:T(8,128)(2,1)S(1)} %copy-done.35, bf16[3,128,1024]{2,1,0:T(8,128)(2,1)S(1)} %copy-done.13, bf16[3,128,1024]{2,1,0:T(8,128)(2,1)S(1)} %copy-done.33, ...), custom_call_target="tpu_custom_call" | custom-call | flops 3221225472 | bytes 6291456 | tf_op jit(solution)/shard_map/pallas_call | solution.py:165
  181.9 5.0 %shard_map.126 = (bf16[3,64,1024]{2,1,0:T(8,128)(2,1)S(1)}, bf16[3,64,1024]{2,1,0:T(8,128)(2,1)}) custom-call(bf16[2,128,1024]{2,1,0:T(8,128)(2,1)S(1)} %collective-permute-done.28.x_ref, bf16[1024,4096]{1,0:T(8,128)(2,1)S(1)} %bitcast.17, bf16[1024,4096]{1,0:T(8,128)(2,1)} %refs_5_.23, bf16[4096,1024]{1,0:T(8,128)(2,1)} %d_ref.23, ...), custom_call_target="tpu_custom_call" | custom-call | flops 805306368 | bytes 6291456 | tf_op jit(solution)/shard_map/pallas_call | solution.py:64
  187.8 4.1 %shard_map.123.refs_2_.refs_7_ = f32[256,1024]{1,0:T(8,128)S(1)} custom-call(bf16[3,128,1024]{2,1,0:T(8,128)(2,1)} %shard_map.122.refs_0_.refs_2_, bf16[3,128,1024]{2,1,0:T(8,128)(2,1)} %collective-permute-done.24.refs_1_.refs_3_, bf16[3,128,1024]{2,1,0:T(8,128)(2,1)} %shard_map.122.refs_0_.refs_2_, ...), custom_call_target="tpu_custom_call" | custom-call | flops 1073741824 | bytes 4194304 | tf_op jit(solution)/shard_map/pallas_call | solution.py:128
  195.4 6.4 %shard_map.136 = (bf16[1024,4096]{1,0:T(8,128)(2,1)}, bf16[1024,4096]{1,0:T(8,128)(2,1)}, bf16[4096,1024]{1,0:T(8,128)(2,1)}) custom-call(bf16[3,64,1024]{2,1,0:T(8,128)(2,1)S(1)} %shard_map.104.refs_0_.refs_2_, bf16[3,64,1024]{2,1,0:T(8,128)(2,1)S(1)} %copy-done.27, ...), custom_call_target="tpu_custom_call", output_to_operand_aliasing={{0}: (10, {}), {1}: (11, {}), {2}: (12, {})} | custom-call | flops 3221225472 | bytes 6291456 | tf_op jit(solution)/shard_map/pallas_call | solution.py:165
  203.6 4.3 %shard_map.135.refs_2_.refs_7_ = f32[128,1024]{1,0:T(8,128)S(1)} custom-call(bf16[3,64,1024]{2,1,0:T(8,128)(2,1)} %shard_map.134.refs_0_.refs_2_.refs_4_, bf16[3,64,1024]{2,1,0:T(8,128)(2,1)S(1)} %copy-done.29, bf16[3,64,1024]{2,1,0:T(8,128)(2,1)} %shard_map.134.refs_0_.refs_2_.refs_4_, bf16[3,64,1024]{2,1,0:T(8,128)(2,1)S(1)} %copy-done.29, ...), custom_call_target="tpu_custom_call" | custom-call | flops 536870912 | bytes 4194304 | tf_op jit(solution)/shard_map/pallas_call | solution.py:128
  217.0 6.4 %shard_map.140 = (bf16[1024,4096]{1,0:T(8,128)(2,1)}, bf16[1024,4096]{1,0:T(8,128)(2,1)}, bf16[4096,1024]{1,0:T(8,128)(2,1)}) custom-call(bf16[3,64,1024]{2,1,0:T(8,128)(2,1)S(1)} %copy-done.19, bf16[3,64,1024]{2,1,0:T(8,128)(2,1)S(1)} %copy-done.25, ...), custom_call_target="tpu_custom_call", output_to_operand_aliasing={{0}: (10, {}), {1}: (11, {}), {2}: (12, {})} | custom-call | flops 3221225472 | bytes 6291456 | tf_op jit(solution)/shard_map/pallas_call | solution.py:165
  235.8 5.5 %shard_map.141 = (bf16[1024,4096]{1,0:T(8,128)(2,1)}, bf16[1024,4096]{1,0:T(8,128)(2,1)}, bf16[4096,1024]{1,0:T(8,128)(2,1)}) custom-call(bf16[3,64,1024]{2,1,0:T(8,128)(2,1)S(1)} %copy-done.17, bf16[3,64,1024]{2,1,0:T(8,128)(2,1)S(1)} %copy-done.23, ...), custom_call_target="tpu_custom_call", output_to_operand_aliasing={{0}: (10, {}), {1}: (11, {}), {2}: (12, {})} | custom-call | flops 3221225472 | bytes 6291456 | tf_op jit(solution)/shard_map/pallas_call | solution.py:165
  244.0 10.7 %collective-permute-done.41 = bf16[128,1024]{1,0:T(8,128)(2,1)S(1)} collective-permute-done((bf16[128,1024]{1,0:T(8,128)(2,1)S(1)}, bf16[128,1024]{1,0:T(8,128)(2,1)S(1)}, u32[]{:S(2)}, u32[]{:S(2)}) %collective-permute-start.41) | collective-permute-done | bytes 262176 | tf_op jit(solution)/shard_map/ppermute | solution.py:200
  (235 shorter events, 114.3 us)
Async XLA Ops:
  17.5 17.8 %collective-permute-start.12 = (bf16[2,128,1024]{2,1,0:T(8,128)(2,1)S(1)}, bf16[2,128,1024]{2,1,0:T(8,128)(2,1)S(1)}, u32[]{:S(2)}, u32[]{:S(2)}) collective-permute-start(bf16[2,128,1024]{2,1,0:T(8,128)(2,1)S(1)} %get-tuple-element.77.x_ref), channel_id=1, source_target_pairs={{0,1},{1,2},{2,3},{3,0},{4,5},{5,6},{6,7},{7,4},{8,9},{9,10},{10,1... | collective-permute-start | bytes 1572872 | tf_op jit(solution)/shard_map/ppermute | solution.py:200
  20.5 24.9 %collective-permute-start.13 = (bf16[2,128,1024]{2,1,0:T(8,128)(2,1)S(1)}, bf16[2,128,1024]{2,1,0:T(8,128)(2,1)S(1)}, u32[]{:S(2)}, u32[]{:S(2)}) collective-permute-start(bf16[2,128,1024]{2,1,0:T(8,128)(2,1)S(1)} %get-tuple-element.77.x_ref), channel_id=1, source_target_pairs={{0,3},{1,0},{2,1},{3,2},{4,7},{5,4},{6,5},{7,6},{8,11},{9,8},{10,9... | collective-permute-start | bytes 1572872 | tf_op jit(solution)/shard_map/ppermute | solution.py:200
  22.7 28.9 %collective-permute-start.6 = (bf16[3,64,1024]{2,1,0:T(8,128)(2,1)S(1)}, bf16[3,64,1024]{2,1,0:T(8,128)(2,1)S(1)}, u32[]{:S(2)}, u32[]{:S(2)}) collective-permute-start(bf16[3,64,1024]{2,1,0:T(8,128)(2,1)S(1)} %add_convert_fusion.9.refs_0_), channel_id=1, source_target_pairs={{0,8},{4,12},{8,0},{12,4},{1,9},{5,13},{9,1},{13,5},{2,10},{6,14},... | collective-permute-start | bytes 1179656 | tf_op jit(solution)/shard_map/ppermute | solution.py:236
  29.0 30.0 %collective-permute-start.3 = (bf16[3,64,1024]{2,1,0:T(8,128)(2,1)S(1)}, bf16[3,64,1024]{2,1,0:T(8,128)(2,1)S(1)}, u32[]{:S(2)}, u32[]{:S(2)}) collective-permute-start(bf16[3,64,1024]{2,1,0:T(8,128)(2,1)S(1)} %add_convert_fusion.11.refs_0_), channel_id=1, source_target_pairs={{0,8},{4,12},{8,0},{12,4},{1,9},{5,13},{9,1},{13,5},{2,10},{6,14},... | collective-permute-start | bytes 1179656 | tf_op jit(solution)/shard_map/ppermute | solution.py:236
  51.5 26.5 %collective-permute-start.21 = (bf16[3,128,1024]{2,1,0:T(8,128)(2,1)S(1)}, bf16[3,128,1024]{2,1,0:T(8,128)(2,1)S(1)}, u32[]{:S(2)}, u32[]{:S(2)}) collective-permute-start(bf16[3,128,1024]{2,1,0:T(8,128)(2,1)S(1)} %get-tuple-element.55), channel_id=1, source_target_pairs={{0,4},{4,0},{8,12},{12,8},{1,5},{5,1},{9,13},{13,9},{2,6},{6,2},{1... | collective-permute-start | bytes 2359304 | tf_op jit(solution)/shard_map/ppermute | solution.py:231
  57.4 22.5 %collective-permute-start.14 = (bf16[3,128,1024]{2,1,0:T(8,128)(2,1)S(1)}, bf16[3,128,1024]{2,1,0:T(8,128)(2,1)S(1)}, u32[]{:S(2)}, u32[]{:S(2)}) collective-permute-start(bf16[3,128,1024]{2,1,0:T(8,128)(2,1)S(1)} %get-tuple-element.49), channel_id=1, source_target_pairs={{0,4},{4,0},{8,12},{12,8},{1,5},{5,1},{9,13},{13,9},{2,6},{6,2},{1... | collective-permute-start | bytes 2359304 | tf_op jit(solution)/shard_map/ppermute | solution.py:231
  71.0 18.8 %collective-permute-start.11 = (bf16[3,64,1024]{2,1,0:T(8,128)(2,1)S(1)}, bf16[3,64,1024]{2,1,0:T(8,128)(2,1)S(1)}, u32[]{:S(2)}, u32[]{:S(2)}) collective-permute-start(bf16[3,64,1024]{2,1,0:T(8,128)(2,1)S(1)} %shard_map.111.refs_0_.refs_2_), channel_id=1, source_target_pairs={{0,4},{4,0},{8,12},{12,8},{1,5},{5,1},{9,13},{13,9},{2,6},{6,2},{1... | collective-permute-start | bytes 1179656 | tf_op jit(solution)/shard_map/ppermute | solution.py:238
  78.3 24.5 %collective-permute-start.22 = (bf16[3,128,1024]{2,1,0:T(8,128)(2,1)S(1)}, bf16[3,128,1024]{2,1,0:T(8,128)(2,1)S(1)}, u32[]{:S(2)}, u32[]{:S(2)}) collective-permute-start(bf16[3,128,1024]{2,1,0:T(8,128)(2,1)S(1)} %add_convert_fusion.refs_0_), channel_id=1, source_target_pairs={{0,8},{4,12},{8,0},{12,4},{1,9},{5,13},{9,1},{13,5},{2,10},{6,14},... | collective-permute-start | bytes 2359304 | tf_op jit(solution)/shard_map/ppermute | solution.py:236
  80.2 35.0 %collective-permute-start.19 = (bf16[3,128,1024]{2,1,0:T(8,128)(2,1)S(1)}, bf16[3,128,1024]{2,1,0:T(8,128)(2,1)S(1)}, u32[]{:S(2)}, u32[]{:S(2)}) collective-permute-start(bf16[3,128,1024]{2,1,0:T(8,128)(2,1)S(1)} %add_convert_fusion.3.refs_0_), channel_id=1, source_target_pairs={{0,8},{4,12},{8,0},{12,4},{1,9},{5,13},{9,1},{13,5},{2,10},{6,14},... | collective-permute-start | bytes 2359304 | tf_op jit(solution)/shard_map/ppermute | solution.py:236
  85.4 30.6 %collective-permute-start.15 = (bf16[3,128,1024]{2,1,0:T(8,128)(2,1)S(1)}, bf16[3,128,1024]{2,1,0:T(8,128)(2,1)S(1)}, u32[]{:S(2)}, u32[]{:S(2)}) collective-permute-start(bf16[3,128,1024]{2,1,0:T(8,128)(2,1)S(1)} %get-tuple-element.51), channel_id=1, source_target_pairs={{0,4},{4,0},{8,12},{12,8},{1,5},{5,1},{9,13},{13,9},{2,6},{6,2},{1... | collective-permute-start | bytes 2359304 | tf_op jit(solution)/shard_map/ppermute | solution.py:231
  102.6 20.2 %collective-permute-start.33 = (bf16[3,64,1024]{2,1,0:T(8,128)(2,1)S(1)}, bf16[3,64,1024]{2,1,0:T(8,128)(2,1)S(1)}, u32[]{:S(2)}, u32[]{:S(2)}) collective-permute-start(bf16[3,64,1024]{2,1,0:T(8,128)(2,1)S(1)} %get-tuple-element.61), channel_id=1, source_target_pairs={{0,4},{4,0},{8,12},{12,8},{1,5},{5,1},{9,13},{13,9},{2,6},{6,2},{1... | collective-permute-start | bytes 1179656 | tf_op jit(solution)/shard_map/ppermute | solution.py:231
  103.5 25.8 %collective-permute-start.23 = (bf16[3,128,1024]{2,1,0:T(8,128)(2,1)S(1)}, bf16[3,128,1024]{2,1,0:T(8,128)(2,1)S(1)}, u32[]{:S(2)}, u32[]{:S(2)}) collective-permute-start(bf16[3,128,1024]{2,1,0:T(8,128)(2,1)S(1)} %shard_map.119.refs_0_.refs_2_), channel_id=1, source_target_pairs={{0,4},{4,0},{8,12},{12,8},{1,5},{5,1},{9,13},{13,9},{2,6},{6,2},{1... | collective-permute-start | bytes 2359304 | tf_op jit(solution)/shard_map/ppermute | solution.py:238
  115.9 30.8 %collective-permute-start.20 = (bf16[3,128,1024]{2,1,0:T(8,128)(2,1)S(1)}, bf16[3,128,1024]{2,1,0:T(8,128)(2,1)S(1)}, u32[]{:S(2)}, u32[]{:S(2)}) collective-permute-start(bf16[3,128,1024]{2,1,0:T(8,128)(2,1)S(1)} %shard_map.117.refs_0_.refs_2_), channel_id=1, source_target_pairs={{0,4},{4,0},{8,12},{12,8},{1,5},{5,1},{9,13},{13,9},{2,6},{6,2},{1... | collective-permute-start | bytes 2359304 | tf_op jit(solution)/shard_map/ppermute | solution.py:238
  116.3 34.7 %collective-permute-start.18 = (bf16[3,128,1024]{2,1,0:T(8,128)(2,1)S(1)}, bf16[3,128,1024]{2,1,0:T(8,128)(2,1)S(1)}, u32[]{:S(2)}, u32[]{:S(2)}) collective-permute-start(bf16[3,128,1024]{2,1,0:T(8,128)(2,1)S(1)} %add_convert_fusion.2.refs_0_), channel_id=1, source_target_pairs={{0,8},{4,12},{8,0},{12,4},{1,9},{5,13},{9,1},{13,5},{2,10},{6,14},... | collective-permute-start | bytes 2359304 | tf_op jit(solution)/shard_map/ppermute | solution.py:236
  122.5 30.7 %collective-permute-start.16 = (bf16[3,128,1024]{2,1,0:T(8,128)(2,1)S(1)}, bf16[3,128,1024]{2,1,0:T(8,128)(2,1)S(1)}, u32[]{:S(2)}, u32[]{:S(2)}) collective-permute-start(bf16[3,128,1024]{2,1,0:T(8,128)(2,1)S(1)} %get-tuple-element.53), channel_id=1, source_target_pairs={{0,4},{4,0},{8,12},{12,8},{1,5},{5,1},{9,13},{13,9},{2,6},{6,2},{1... | collective-permute-start | bytes 2359304 | tf_op jit(solution)/shard_map/ppermute | solution.py:231
  122.9 22.3 %collective-permute-start.37 = (bf16[3,64,1024]{2,1,0:T(8,128)(2,1)S(1)}, bf16[3,64,1024]{2,1,0:T(8,128)(2,1)S(1)}, u32[]{:S(2)}, u32[]{:S(2)}) collective-permute-start(bf16[3,64,1024]{2,1,0:T(8,128)(2,1)S(1)} %add_convert_fusion.6.refs_0_), channel_id=1, source_target_pairs={{0,8},{4,12},{8,0},{12,4},{1,9},{5,13},{9,1},{13,5},{2,10},{6,14},... | collective-permute-start | bytes 1179656 | tf_op jit(solution)/shard_map/ppermute | solution.py:236
  129.3 43.1 %collective-permute-start.36 = (bf16[3,64,1024]{2,1,0:T(8,128)(2,1)}, bf16[3,64,1024]{2,1,0:T(8,128)(2,1)}, u32[]{:S(2)}, u32[]{:S(2)}) collective-permute-start(bf16[3,64,1024]{2,1,0:T(8,128)(2,1)} %add_convert_fusion.5.refs_0_), channel_id=1, source_target_pairs={{0,8},{4,12},{8,0},{12,4},{1,9},{5,13},{9,1},{13,5},{2,10},{6,14},... | collective-permute-start | bytes 1179656 | tf_op jit(solution)/shard_map/ppermute | solution.py:236
  145.1 34.3 %collective-permute-start.34 = (bf16[3,64,1024]{2,1,0:T(8,128)(2,1)}, bf16[3,64,1024]{2,1,0:T(8,128)(2,1)}, u32[]{:S(2)}, u32[]{:S(2)}) collective-permute-start(bf16[3,64,1024]{2,1,0:T(8,128)(2,1)} %get-tuple-element.63), channel_id=1, source_target_pairs={{0,4},{4,0},{8,12},{12,8},{1,5},{5,1},{9,13},{13,9},{2,6},{6,2},{1... | collective-permute-start | bytes 1179656 | tf_op jit(solution)/shard_map/ppermute | solution.py:231
  153.0 34.8 %collective-permute-start.24 = (bf16[3,128,1024]{2,1,0:T(8,128)(2,1)}, bf16[3,128,1024]{2,1,0:T(8,128)(2,1)}, u32[]{:S(2)}, u32[]{:S(2)}) collective-permute-start(bf16[3,128,1024]{2,1,0:T(8,128)(2,1)} %shard_map.122.refs_0_.refs_2_), channel_id=1, source_target_pairs={{0,4},{4,0},{8,12},{12,8},{1,5},{5,1},{9,13},{13,9},{2,6},{6,2},{1... | collective-permute-start | bytes 2359304 | tf_op jit(solution)/shard_map/ppermute | solution.py:238
  154.5 37.5 %collective-permute-start.17 = (bf16[3,128,1024]{2,1,0:T(8,128)(2,1)}, bf16[3,128,1024]{2,1,0:T(8,128)(2,1)}, u32[]{:S(2)}, u32[]{:S(2)}) collective-permute-start(bf16[3,128,1024]{2,1,0:T(8,128)(2,1)} %add_convert_fusion.1.refs_0_), channel_id=1, source_target_pairs={{0,8},{4,12},{8,0},{12,4},{1,9},{5,13},{9,1},{13,5},{2,10},{6,14},... | collective-permute-start | bytes 2359304 | tf_op jit(solution)/shard_map/ppermute | solution.py:236
  181.3 26.5 %collective-permute-start.35 = (bf16[3,64,1024]{2,1,0:T(8,128)(2,1)}, bf16[3,64,1024]{2,1,0:T(8,128)(2,1)}, u32[]{:S(2)}, u32[]{:S(2)}) collective-permute-start(bf16[3,64,1024]{2,1,0:T(8,128)(2,1)} %add_convert_fusion.4.refs_0_), channel_id=1, source_target_pairs={{0,8},{4,12},{8,0},{12,4},{1,9},{5,13},{9,1},{13,5},{2,10},{6,14},... | collective-permute-start | bytes 1179656 | tf_op jit(solution)/shard_map/ppermute | solution.py:236
  187.6 22.8 %collective-permute-start.29 = (bf16[3,64,1024]{2,1,0:T(8,128)(2,1)}, bf16[3,64,1024]{2,1,0:T(8,128)(2,1)}, u32[]{:S(2)}, u32[]{:S(2)}) collective-permute-start(bf16[3,64,1024]{2,1,0:T(8,128)(2,1)} %get-tuple-element.57), channel_id=1, source_target_pairs={{0,4},{4,0},{8,12},{12,8},{1,5},{5,1},{9,13},{13,9},{2,6},{6,2},{1... | collective-permute-start | bytes 1179656 | tf_op jit(solution)/shard_map/ppermute | solution.py:231
  195.0 28.4 %collective-permute-start.25 = (bf16[3,128,1024]{2,1,0:T(8,128)(2,1)S(1)}, bf16[3,128,1024]{2,1,0:T(8,128)(2,1)S(1)}, u32[]{:S(2)}, u32[]{:S(2)}) collective-permute-start(bf16[3,128,1024]{2,1,0:T(8,128)(2,1)S(1)} %shard_map.124.refs_0_.refs_2_), channel_id=1, source_target_pairs={{0,4},{4,0},{8,12},{12,8},{1,5},{5,1},{9,13},{13,9},{2,6},{6,2},{1... | collective-permute-start | bytes 2359304 | tf_op jit(solution)/shard_map/ppermute | solution.py:238
  234.8 19.9 %collective-permute-start.41 = (bf16[128,1024]{1,0:T(8,128)(2,1)S(1)}, bf16[128,1024]{1,0:T(8,128)(2,1)S(1)}, u32[]{:S(2)}, u32[]{:S(2)}) collective-permute-start(bf16[128,1024]{1,0:T(8,128)(2,1)S(1)} %convert_element_type.197), channel_id=1, source_target_pairs={{0,2},{1,3},{2,0},{3,1},{4,6},{5,7},{6,4},{7,5},{8,10},{9,11},{10,... | collective-permute-start | bytes 786440 | tf_op jit(solution)/shard_map/ppermute | solution.py:200
  (66 other events, 585.2 us)

commit v3 on v2

--- a/solution.py
+++ b/solution.py
@@ -11,7 +11,7 @@
 STEP = 256
 CONTRACT_ROWS = (((0,), (0,)), ((), ()))
 CONTRACT_COLUMNS = (((1,), (1,)), ((), ()))
-PARAMS = pltpu.CompilerParams(vmem_limit_bytes=40 * 2**20)
+PARAMS = pltpu.CompilerParams(vmem_limit_bytes=56 * 2**20)
 
 
 def masked(weight, lines):
@@ -80,6 +80,49 @@
     )(x, gate, up, down, *lines, *after)
 
 
+def join_kernel(n, *refs):
+    out_ref = refs[-1]
+    half = refs[0].shape[1] // 2
+    for i in range(n):
+        out_ref[:, i * half : (i + 1) * half] = refs[i][:, :half]
+        out_ref[:, (n + i) * half : (n + i + 1) * half] = refs[i][:, half:]
+
+
+def joined(blocks, after):
+    n = len(blocks)
+    two, count, height = blocks[0].shape
+    step = min(2 * STEP, height)
+    return pl.pallas_call(
+        functools.partial(join_kernel, n),
+        out_shape=jax.ShapeDtypeStruct((two, n * count, height), jnp.bfloat16),
+        grid=(height // step,),
+        in_specs=[pl.BlockSpec((two, count, step), lambda j: (0, 0, j))] * n + [ANY] * len(after),
+        out_specs=pl.BlockSpec((two, n * count, step), lambda j: (0, 0, j)),
+        compiler_params=PARAMS,
+        cost_estimate=cost(0, 4 * n * two * count * height),
+    )(*blocks, *after)
+
+
+def add_kernel(left_ref, right_ref, *refs):
+    out_ref = refs[-1]
+    out_ref[...] = (left_ref[...].astype(jnp.float32) + right_ref[...].astype(jnp.float32)).astype(jnp.bfloat16)
+
+
+def added(left, right, after):
+    three, count, size = left.shape
+    step = min(2 * STEP, size)
+    spec = pl.BlockSpec((three, count, step), lambda j: (0, 0, j))
+    return pl.pallas_call(
+        add_kernel,
+        out_shape=jax.ShapeDtypeStruct(left.shape, jnp.bfloat16),
+        grid=(size // step,),
+        in_specs=[spec] * 2 + [ANY] * len(after),
+        out_specs=spec,
+        compiler_params=PARAMS,
+        cost_estimate=cost(3 * count * size, 18 * count * size),
+    )(left, right, *after)
+
+
 def delta_kernel(n, *refs):
     out_ref = refs[-1]
     gate, up, hidden_delta = (
@@ -107,41 +150,43 @@
     )(*parts, *after)
 
 
-def term_kernel(first, *refs):
-    gd_mine, gd_theirs, ud_mine, ud_theirs, g_ref, u_ref, l_ref = refs[:7]
+def term_kernel(first, n, *refs):
+    g_ref, u_ref, l_ref = refs[2 * n : 2 * n + 3]
     out_ref = refs[-1]
-    gate_delta = jnp.concatenate([gd_mine[0], gd_theirs[0]], axis=0)
-    up_delta = jnp.concatenate([ud_mine[0], ud_theirs[0]], axis=0)
+    gate_delta = jnp.concatenate([r[0] for r in refs[:n]], axis=0)
+    up_delta = jnp.concatenate([r[0] for r in refs[n : 2 * n]], axis=0)
     value = behind(gate_delta, masked(g_ref[...], l_ref[...])) + behind(up_delta, masked(u_ref[...], l_ref[...]))
-    out_ref[...] = value if first else refs[7][...] + value
-
-
-def add_term(pair, weights, lines, k, size, term):
+    out_ref[...] = value if first else refs[2 * n + 3][...] + value
+
+
+def add_term(parts, weights, lines, k, size, term, after):
     gate, up, _ = weights
     height = gate.shape[0]
-    count = 2 * pair[0].shape[1]
+    count = sum(p.shape[1] for p in parts)
     step = min(STEP, height)
     held = pl.BlockSpec((count, step), lambda j: (0, j))
     rows = pl.BlockSpec((step, size), lambda j: (j, k))
-    pieces = [pl.BlockSpec((1, count // 2, size), lambda j, i=i: (i, 0, 0)) for i in (1, 1, 2, 2)]
+    pieces = [pl.BlockSpec((1, p.shape[1], size), lambda j, i=i: (i, 0, 0)) for i in (1, 2) for p in parts]
     extra = [] if term is None else [term]
     return pl.pallas_call(
-        functools.partial(term_kernel, term is None),
+        functools.partial(term_kernel, term is None, len(parts)),
         out_shape=jax.ShapeDtypeStruct((count, height), jnp.float32),
         grid=(height // step,),
         in_specs=pieces
         + [rows, rows, pl.BlockSpec((step // BLK, 1, size), lambda j: (j, 0, k))]
-        + [held] * len(extra),
+        + [held] * len(extra)
+        + [ANY] * len(after),
         out_specs=held,
         compiler_params=PARAMS,
         cost_estimate=cost(4 * count * height * size, 4 * height * size),
-    )(pair[0], pair[1], pair[0], pair[1], gate, up, lines[0], *extra)
+    )(*parts, *parts, gate, up, lines[0], *extra, *after)
 
 
 def gradient_kernel(n, *refs):
     parts = refs[:n]
     tokens_ref, cotangent_ref, gl_ref, dl_ref = refs[n : n + 4]
-    gate_ref, up_ref, down_ref = refs[-3:]
+    gate_ref, up_ref, down_ref, token_ref = refs[-4:]
+    token_ref[...] = jnp.zeros_like(token_ref)
 
     def put(ref, product, lines):
         rows, columns = product.shape
@@ -154,7 +199,7 @@
     put(down_ref, outer(hidden, cotangent_ref[...]), dl_ref[...])
 
 
-def gradients(parts, tokens_t, cotangent, lines, k, size, width, into):
+def gradients(parts, tokens_t, cotangent, lines, k, size, width, into, after):
     height, depth = tokens_t.shape
     step = min(STEP, size)
     base = k * size // step
@@ -164,7 +209,7 @@
     wide = jax.ShapeDtypeStruct((height, width), jnp.bfloat16)
     return pl.pallas_call(
         functools.partial(gradient_kernel, n),
-        out_shape=(wide, wide, jax.ShapeDtypeStruct((width, height), jnp.bfloat16)),
+        out_shape=(wide, wide, jax.ShapeDtypeStruct((width, height), jnp.bfloat16), jax.ShapeDtypeStruct((8, BLK), jnp.float32)),
         grid=(size // step,),
         in_specs=[pl.BlockSpec((3, p.shape[1], step), lambda j: (0, 0, j)) for p in parts]
         + [
@@ -173,12 +218,12 @@
             pl.BlockSpec((height // BLK, 1, step), lambda j: (0, 0, base + j)),
             pl.BlockSpec((step // BLK, 1, height), lambda j: (base + j, 0, 0)),
         ]
-        + [ANY] * len(into),
-        out_specs=(columns, columns, down_rows),
+        + [ANY] * (len(into) + len(after)),
+        out_specs=(columns, columns, down_rows, pl.BlockSpec((8, BLK), lambda j: (0, 0))),
         input_output_aliases={n + 4 + i: i for i in range(len(into))},
         compiler_params=PARAMS,
         cost_estimate=cost(6 * height * depth * size, 6 * height * size),
-    )(*parts, tokens_t, cotangent, *lines, *into)
+    )(*parts, tokens_t, cotangent, *lines, *into, *after)
 
 
 def on_device(n_row, n_col, tokens, cotangent, gate_weight, up_weight, down_weight, gate_keep, down_keep):
@@ -200,59 +245,69 @@
         return lax.ppermute(value, "col", [(i, (i + s) % n_col) for i in range(n_col)])
 
     both = core_order(jnp.stack([tokens, cotangent]))
-    block = {0: both}
-    for s in range(1, n_col // 2 + 1):
-        block[s] = shifted(block[s - 1], 1)
-        if n_col - s > n_col // 2:
-            block[n_col - s] = shifted(block[(n_col - s + 1) % n_col], -1)
-    near = [s for s in dict.fromkeys((1, n_col - 1)) if 0 < s < n_col]
-    far = [s for s in range(2, n_col - 1)]
-    shifts = [g for g in ([0], near, far) if g]
-    groups = [
-        jnp.concatenate([block[s][:, :half] for s in g] + [block[s][:, half:] for s in g], axis=1) for g in shifts
-    ]
+    others = [shifted(both, s) for s in range(1, n_col)]
+    groups = [both]
+
+    last = []
+
+    def chained(kernel, *operands):
+        result = kernel(*operands, list(last))
+        last[:] = [result[-1] if isinstance(result, (tuple, list)) else result]
+        return result
+
+    pending, summed, pairs = {}, {}, {}
+
+    def multiply(u):
+        g, k = u
+        mine, theirs = chained(products, groups[g], weights, lines, k, size)
+        pending[u] = (mine, lax.ppermute(theirs, "row", swap))
+
+    def combine(u):
+        mine = chained(added, *pending[u])
+        summed[u] = [mine]
+        for c in range(1, chips):
+            summed[u].append(lax.ppermute(mine, "row", [(i, (i + 2 * c) % n_row) for i in range(n_row)]))
+
+    def activate(u):
+        result = chained(deltas, summed[u])
+        pairs[u] = (result, lax.ppermute(result, "row", swap))
+
+    own = [(0, k) for k in range(chunks)]
+    rest = [(1, k) for k in range(chunks)] if others else []
+    for i in range(chunks + 1):
+        if i < chunks:
+            multiply(own[i])
+        if i > 0:
+            combine(own[i - 1])
+    for u in own[:-1]:
+        activate(u)
+    if rest:
+        groups.append(chained(joined, others))
+        multiply(rest[0])
+        for i in range(1, chunks + 1):
+            if i < chunks:
+                multiply(rest[i])
+            combine(rest[i - 1])
+    for u in own[-1:]:
+        if u not in pairs:
+            activate(u)
     rows = jnp.concatenate(groups, axis=1)
     tokens_t = rows[0].T
-
-    order = [(0, k) for k in range(chunks)]
-    if len(groups) > 1:
-        order += [(1, 0)] + [(1, 1)] * (chunks > 1)
-    if len(groups) > 2:
-        for k in range(chunks):
-            order += [(2, k)] + [(1, k + 2)] * (k + 2 < chunks)
-    elif len(groups) > 1:
-        order += [(1, k) for k in range(2, chunks)]
-
-    mine_of, pairs, terms = [], {}, [None] * len(groups)
-    seen, into, ready = [0] * chunks, (), {}
-    for at, (g, k) in enumerate(order):
-        after = [mine_of[at - 2]] if at >= 2 else []
-        mine, theirs = products(groups[g], weights, lines, k, size, after)
-        came = lax.ppermute(theirs, "row", swap)
-        mine = (mine.astype(jnp.float32) + came.astype(jnp.float32)).astype(jnp.bfloat16)
-        mine_of.append(mine)
-        parts = [mine]
-        for c in range(1, chips):
-            parts.append(lax.ppermute(mine, "row", [(i, (i + 2 * c) % n_row) for i in range(n_row)]))
-        result = deltas(parts, ready.get(at, []))
-        pairs[g, k] = (result, lax.ppermute(result, "row", swap))
-        terms[g] = add_term(pairs[g, k], weights, lines, k, size, terms[g])
-        done = [terms[g]]
-        seen[k] += 1
-        if seen[k] == len(groups):
-            pieces = [p for gg in range(len(groups)) for p in pairs[gg, k]]
-            into = gradients(pieces, tokens_t, rows[1], lines, k, size, width, into)
-            done += list(into)
-        ready[at + 2] = done
-
-    total = terms[0]
-    for g in range(1, len(groups)):
-        sent = terms[g].astype(jnp.bfloat16)
-        middle = half * len(shifts[g])
-        for at, s in enumerate(shifts[g]):
-            low = at * half
-            piece = jnp.concatenate([sent[low : low + half], sent[middle + low : middle + low + half]], axis=0)
-            total = total + shifted(piece, -s).astype(jnp.float32)
+    term, into = None, ()
+    for k in range(chunks):
+        if rest:
+            activate(rest[k])
+        pieces = [p for g in range(len(groups)) for p in pairs[g, k]]
+        term = chained(add_term, pieces, weights, lines, k, size, term)
+        *into, _ = chained(gradients, pieces, tokens_t, rows[1], lines, k, size, width, into)
+
+    total = term[:own_rows]
+    sent = term[own_rows:].astype(jnp.bfloat16)
+    middle = half * len(others)
+    for s in range(1, n_col):
+        low = (s - 1) * half
+        piece = jnp.concatenate([sent[low : low + half], sent[middle + low : middle + low + half]], axis=0)
+        total = total + shifted(piece, -s).astype(jnp.float32)
     return (core_order(total[None])[0].astype(jnp.bfloat16), *into)
 
 

time: 258 us -> 316 us (1.22)
  waiting for transfers between devices: 53.9 us -> 90.6 us
  Pallas kernels: 142 us -> 160 us
  local copies, waits for them, and re-layouts: 16.3 us -> 23 us
  other arithmetic: 12.8 us -> 7.89 us
    ppermute x36 -> x24, waiting for transfers between devices: 29.3 us -> 67.9 us  [the longest x8 59.5 us: combine(): lax.ppermute(mine, 'row', [(i, (i + 2 * c) % n_row) for i in range(n_row)])]
    pallas_call x12 -> x8, Pallas kernels: 15.8 us -> 29.7 us  [deltas(): pl.pallas_call(functools.partial(delta_kernel, len(parts)), out_shape=jax...]
    ppermute x6, starting transfers between devices: 10.1 us -> 19 us  [shifted(): lax.ppermute(value, 'col', [(i, (i + s) % n_col) for i in range(n_col)])]
    convert_element_type x14 -> x0, other arithmetic: 7.81 us -> none  [the longest x12 7.71 us: on_device(): (mine.astype(jnp.float32) + came.astype(jnp.float32)).astype(jnp.bfloat16)]
    ppermute x36 -> x24, starting transfers between devices: 18.8 us -> 12.4 us  [the longest x8 9.41 us: combine(): lax.ppermute(mine, 'row', [(i, (i + 2 * c) % n_row) for i in range(n_row)])]
    unnamed x100 -> x84, local copies, waits for them, and re-layouts: 13.2 us -> 19 us
    pallas_call x4, Pallas kernels: 24.6 us -> 29.6 us  [gradients(): pl.pallas_call(functools.partial(gradient_kernel, n), out_shape=(wide, wi...]
    pallas_call x12 -> x8, Pallas kernels: 54.9 us -> 51.8 us  [products(): pl.pallas_call(product_kernel, out_shape=(out, out), grid=(size // step,)...]
  transfers between devices with their start and end apart: 42 -> 30, of which waited for: 8 -> 13; matrix products, arithmetic and copies ran while one was open for 4% -> 1% of each run, Pallas kernels for 54% -> 39%
where the time goes in v3:
time: 316 us; the launch traced here: 313 us
  Pallas kernels  160 us (51%)
  waiting for transfers between devices  90.6 us (29%)
  starting transfers between devices  31.4 us (10%)
  local copies, waits for them, and re-layouts  23 us (7%)
  other arithmetic  7.89 us (2%)
    ppermute x8, waiting for transfers between devices, combine(): lax.ppermute(mine, 'row', [(i, (i + 2 * c) % n_row) for i in range(n_row)])  59.5 us
    pallas_call x8, Pallas kernels, products(): pl.pallas_call(product_kernel, out_shape=(out, out), grid=(size // step,)...  51.8 us
    pallas_call x8, Pallas kernels, deltas(): pl.pallas_call(functools.partial(delta_kernel, len(parts)), out_shape=jax...  29.7 us
    pallas_call x4, Pallas kernels, gradients(): pl.pallas_call(functools.partial(gradient_kernel, n), out_shape=(wide, wi...  29.6 us
    pallas_call x4, Pallas kernels, add_term(): pl.pallas_call(functools.partial(term_kernel, term is None, len(parts)),...  27.8 us
    ppermute x6, waiting for transfers between devices, shifted(): lax.ppermute(value, 'col', [(i, (i + s) % n_col) for i in range(n_col)])  22.7 us
    unnamed x84, local copies, waits for them, and re-layouts  19 us
    ppermute x6, starting transfers between devices, shifted(): lax.ppermute(value, 'col', [(i, (i + s) % n_col) for i in range(n_col)])  19 us
  transfers between devices with their start and end apart: 30, of which 13 were waited for; matrix products, arithmetic and copies ran while one was open for 1% of the time, Pallas kernels for 39%

profile of v3, /device:TPU:0, one launch (start us, length us, event | category | flops | bytes accessed | tf_op | source)
XLA Modules:
  0.0 313.3 jit_solution(7681168099635845921)
XLA Ops:
  5.9 5.6 %shard_map.102 = (bf16[3,64,1024]{2,1,0:T(8,128)(2,1)}, bf16[3,64,1024]{2,1,0:T(8,128)(2,1)}) custom-call(bf16[2,128,1024]{2,1,0:T(8,128)(2,1)} %fusion.3.x_ref, bf16[1024,4096]{1,0:T(8,128)(2,1)} %refs_8_.7, bf16[1024,4096]{1,0:T(8,128)(2,1)} %refs_9_.7, bf16[4096,1024]{1,0:T(8,128)(2,1)} %d_ref.15, ...), custom_call_target="tpu_custom_call" | custom-call | flops 805306368 | bytes 6291456 | tf_op jit(solution)/shard_map/pallas_call | solution.py:64
  11.9 5.8 %shard_map.103 = (bf16[3,64,1024]{2,1,0:T(8,128)(2,1)}, bf16[3,64,1024]{2,1,0:T(8,128)(2,1)}) custom-call(bf16[2,128,1024]{2,1,0:T(8,128)(2,1)} %fusion.3.x_ref, bf16[1024,4096]{1,0:T(8,128)(2,1)} %refs_8_.7, bf16[1024,4096]{1,0:T(8,128)(2,1)} %refs_9_.7, bf16[4096,1024]{1,0:T(8,128)(2,1)} %d_ref.15, ...), custom_call_target="tpu_custom_call" | custom-call | flops 805306368 | bytes 6291456 | tf_op jit(solution)/shard_map/pallas_call | solution.py:64
  20.5 5.8 %shard_map.105 = (bf16[3,64,1024]{2,1,0:T(8,128)(2,1)}, bf16[3,64,1024]{2,1,0:T(8,128)(2,1)}) custom-call(bf16[2,128,1024]{2,1,0:T(8,128)(2,1)} %fusion.3.x_ref, bf16[1024,4096]{1,0:T(8,128)(2,1)} %refs_8_.7, bf16[1024,4096]{1,0:T(8,128)(2,1)} %refs_9_.7, bf16[4096,1024]{1,0:T(8,128)(2,1)} %d_ref.15, ...), custom_call_target="tpu_custom_call" | custom-call | flops 805306368 | bytes 6291456 | tf_op jit(solution)/shard_map/pallas_call | solution.py:64
  29.5 5.8 %shard_map.107 = (bf16[3,64,1024]{2,1,0:T(8,128)(2,1)}, bf16[3,64,1024]{2,1,0:T(8,128)(2,1)}) custom-call(bf16[2,128,1024]{2,1,0:T(8,128)(2,1)} %fusion.3.x_ref, bf16[1024,4096]{1,0:T(8,128)(2,1)} %refs_8_.7, bf16[1024,4096]{1,0:T(8,128)(2,1)} %refs_9_.7, bf16[4096,1024]{1,0:T(8,128)(2,1)} %d_ref.15, ...), custom_call_target="tpu_custom_call" | custom-call | flops 805306368 | bytes 6291456 | tf_op jit(solution)/shard_map/pallas_call | solution.py:64
  68.6 7.8 %collective-permute-done.6.refs_1_ = bf16[2,128,1024]{2,1,0:T(8,128)(2,1)S(1)} collective-permute-done((bf16[2,128,1024]{2,1,0:T(8,128)(2,1)S(1)}, bf16[2,128,1024]{2,1,0:T(8,128)(2,1)S(1)}, u32[]{:S(2)}, u32[]{:S(2)}) %collective-permute-start.6) | collective-permute-done | bytes 524320 | tf_op jit(solution)/shard_map/ppermute | solution.py:245
  80.3 7.0 %shard_map.114 = (bf16[3,192,1024]{2,1,0:T(8,128)(2,1)}, bf16[3,192,1024]{2,1,0:T(8,128)(2,1)}) custom-call(bf16[2,384,1024]{2,1,0:T(8,128)(2,1)} %shard_map.113.x_ref.refs_0_, bf16[1024,4096]{1,0:T(8,128)(2,1)} %refs_8_.7, bf16[1024,4096]{1,0:T(8,128)(2,1)} %refs_9_.7, bf16[4096,1024]{1,0:T(8,128)(2,1)} %d_ref.15, ...), custom_call_target="tpu_custom_call" | custom-call | flops 2415919104 | bytes 6291456 | tf_op jit(solution)/shard_map/pallas_call | solution.py:64
  87.3 7.3 %shard_map.115 = (bf16[3,192,1024]{2,1,0:T(8,128)(2,1)}, bf16[3,192,1024]{2,1,0:T(8,128)(2,1)}) custom-call(bf16[2,384,1024]{2,1,0:T(8,128)(2,1)} %shard_map.113.x_ref.refs_0_, bf16[1024,4096]{1,0:T(8,128)(2,1)} %refs_8_.7, bf16[1024,4096]{1,0:T(8,128)(2,1)} %refs_9_.7, bf16[4096,1024]{1,0:T(8,128)(2,1)} %d_ref.15, ...), custom_call_target="tpu_custom_call" | custom-call | flops 2415919104 | bytes 6291456 | tf_op jit(solution)/shard_map/pallas_call | solution.py:64
  98.7 7.2 %shard_map.117 = (bf16[3,192,1024]{2,1,0:T(8,128)(2,1)}, bf16[3,192,1024]{2,1,0:T(8,128)(2,1)}) custom-call(bf16[2,384,1024]{2,1,0:T(8,128)(2,1)} %shard_map.113.x_ref.refs_0_, bf16[1024,4096]{1,0:T(8,128)(2,1)} %refs_8_.7, bf16[1024,4096]{1,0:T(8,128)(2,1)} %refs_9_.7, bf16[4096,1024]{1,0:T(8,128)(2,1)} %d_ref.15, ...), custom_call_target="tpu_custom_call" | custom-call | flops 2415919104 | bytes 6291456 | tf_op jit(solution)/shard_map/pallas_call | solution.py:64
  109.7 7.3 %shard_map.119 = (bf16[3,192,1024]{2,1,0:T(8,128)(2,1)}, bf16[3,192,1024]{2,1,0:T(8,128)(2,1)}) custom-call(bf16[2,384,1024]{2,1,0:T(8,128)(2,1)} %shard_map.113.x_ref.refs_0_, bf16[1024,4096]{1,0:T(8,128)(2,1)} %refs_8_.7, bf16[1024,4096]{1,0:T(8,128)(2,1)} %refs_9_.7, bf16[4096,1024]{1,0:T(8,128)(2,1)} %d_ref.15, ...), custom_call_target="tpu_custom_call" | custom-call | flops 2415919104 | bytes 6291456 | tf_op jit(solution)/shard_map/pallas_call | solution.py:64
  126.7 27.1 %collective-permute-done.4.refs_1_ = bf16[3,64,1024]{2,1,0:T(8,128)(2,1)S(1)} collective-permute-done((bf16[3,64,1024]{2,1,0:T(8,128)(2,1)S(1)}, bf16[3,64,1024]{2,1,0:T(8,128)(2,1)S(1)}, u32[]{:S(2)}, u32[]{:S(2)}) %collective-permute-start.4) | collective-permute-done | bytes 393248 | tf_op jit(solution)/shard_map/ppermute | solution.py:269
  159.0 4.3 %shard_map.123.refs_2_.refs_6_.refs_11_ = bf16[3,192,1024]{2,1,0:T(8,128)(2,1)} custom-call(bf16[3,192,1024]{2,1,0:T(8,128)(2,1)} %shard_map.116.refs_0_, bf16[3,192,1024]{2,1,0:T(8,128)(2,1)} %copy-done.22, bf16[3,64,1024]{2,1,0:T(8,128)(2,1)} %shard_map.122.refs_2_.refs_0_.refs_4_), custom_call_target="tpu_custom_call" | custom-call | flops 11796480 | bytes 3538944 | tf_op jit(solution)/shard_map/pallas_call | solution.py:142
  169.6 6.7 %shard_map.124.refs_8_.refs_11_ = f32[512,1024]{1,0:T(8,128)} custom-call(bf16[3,64,1024]{2,1,0:T(8,128)(2,1)} %shard_map.110.refs_2_.refs_0_.refs_4_, bf16[3,64,1024]{2,1,0:T(8,128)(2,1)} %copy-done.21, bf16[3,192,1024]{2,1,0:T(8,128)(2,1)} %shard_map.123.refs_2_.refs_6_.refs_11_, bf16[3,192,1024]{2,1,0:T(8,128)(2,1)} %copy-done.14, ...), custom_call_target="tpu_custom_call" | custom-call | flops 2147483648 | bytes 4194304 | tf_op jit(solution)/shard_map/pallas_call | solution.py:171
  176.2 7.4 %shard_map.125 = (bf16[1024,4096]{1,0:T(8,128)(2,1)}, bf16[1024,4096]{1,0:T(8,128)(2,1)}, bf16[4096,1024]{1,0:T(8,128)(2,1)}, f32[8,128]{1,0:T(8,128)}) custom-call(bf16[3,64,1024]{2,1,0:T(8,128)(2,1)} %shard_map.110.refs_2_.refs_0_.refs_4_, bf16[3,64,1024]{2,1,0:T(8,128)(2,1)} %copy-done.21, bf16[3,192,1024]{2,1,0:T(8,128)(2,1)} %shard_map.123.refs_2_.refs_6_.refs_11_, ...), custom_call_target="tpu_custom_call" | custom-call | flops 3221225472 | bytes 6291456 | tf_op jit(solution)/shard_map/pallas_call | solution.py:210
  183.6 8.2 %collective-permute-done.20.refs_1_ = bf16[3,192,1024]{2,1,0:T(8,128)(2,1)} collective-permute-done((bf16[3,192,1024]{2,1,0:T(8,128)(2,1)S(1)}, bf16[3,192,1024]{2,1,0:T(8,128)(2,1)}, u32[]{:S(2)}, u32[]{:S(2)}) %collective-permute-start.20) | collective-permute-done | bytes 1179680 | tf_op jit(solution)/shard_map/ppermute | solution.py:269
  201.0 7.1 %shard_map.127.refs_11_ = f32[512,1024]{1,0:T(8,128)} custom-call(bf16[3,64,1024]{2,1,0:T(8,128)(2,1)} %shard_map.111.refs_2_.refs_0_.refs_4_, bf16[3,64,1024]{2,1,0:T(8,128)(2,1)} %copy-done.16, bf16[3,192,1024]{2,1,0:T(8,128)(2,1)} %shard_map.126.refs_2_.refs_6_.refs_12_, bf16[3,192,1024]{2,1,0:T(8,128)(2,1)} %copy-done.4, ...), custom_call_target="tpu_custom_call" | custom-call | flops 2147483648 | bytes 4194304 | tf_op jit(solution)/shard_map/pallas_call | solution.py:171
  208.0 7.4 %shard_map.128 = (bf16[1024,4096]{1,0:T(8,128)(2,1)}, bf16[1024,4096]{1,0:T(8,128)(2,1)}, bf16[4096,1024]{1,0:T(8,128)(2,1)}, f32[8,128]{1,0:T(8,128)}) custom-call(bf16[3,64,1024]{2,1,0:T(8,128)(2,1)} %shard_map.111.refs_2_.refs_0_.refs_4_, bf16[3,64,1024]{2,1,0:T(8,128)(2,1)} %copy-done.16, ...), custom_call_target="tpu_custom_call", output_to_operand_aliasing={{0}: (8, {}), {1}: (9, {}), {2}: (10, {})} | custom-call | flops 3221225472 | bytes 6291456 | tf_op jit(solution)/shard_map/pallas_call | solution.py:210
  215.4 8.8 %collective-permute-done.18.refs_1_ = bf16[3,192,1024]{2,1,0:T(8,128)(2,1)S(1)} collective-permute-done((bf16[3,192,1024]{2,1,0:T(8,128)(2,1)S(1)}, bf16[3,192,1024]{2,1,0:T(8,128)(2,1)S(1)}, u32[]{:S(2)}, u32[]{:S(2)}) %collective-permute-start.18) | collective-permute-done | bytes 1179680 | tf_op jit(solution)/shard_map/ppermute | solution.py:269
  234.5 7.0 %shard_map.130.refs_11_ = f32[512,1024]{1,0:T(8,128)} custom-call(bf16[3,64,1024]{2,1,0:T(8,128)(2,1)} %shard_map.112.refs_3_.refs_0_.refs_4_, bf16[3,64,1024]{2,1,0:T(8,128)(2,1)} %copy-done.17, bf16[3,192,1024]{2,1,0:T(8,128)(2,1)} %shard_map.129.refs_2_.refs_6_.refs_12_, bf16[3,192,1024]{2,1,0:T(8,128)(2,1)} %copy-done.5, ...), custom_call_target="tpu_custom_call" | custom-call | flops 2147483648 | bytes 4194304 | tf_op jit(solution)/shard_map/pallas_call | solution.py:171
  241.5 7.4 %shard_map.131 = (bf16[1024,4096]{1,0:T(8,128)(2,1)}, bf16[1024,4096]{1,0:T(8,128)(2,1)}, bf16[4096,1024]{1,0:T(8,128)(2,1)}, f32[8,128]{1,0:T(8,128)}) custom-call(bf16[3,64,1024]{2,1,0:T(8,128)(2,1)} %shard_map.112.refs_3_.refs_0_.refs_4_, bf16[3,64,1024]{2,1,0:T(8,128)(2,1)} %copy-done.17, ...), custom_call_target="tpu_custom_call", output_to_operand_aliasing={{0}: (8, {}), {1}: (9, {}), {2}: (10, {})} | custom-call | flops 3221225472 | bytes 6291456 | tf_op jit(solution)/shard_map/pallas_call | solution.py:210
  248.9 8.7 %collective-permute-done.16.refs_1_ = bf16[3,192,1024]{2,1,0:T(8,128)(2,1)S(1)} collective-permute-done((bf16[3,192,1024]{2,1,0:T(8,128)(2,1)S(1)}, bf16[3,192,1024]{2,1,0:T(8,128)(2,1)S(1)}, u32[]{:S(2)}, u32[]{:S(2)}) %collective-permute-start.16) | collective-permute-done | bytes 1179680 | tf_op jit(solution)/shard_map/ppermute | solution.py:269
  267.5 7.0 %shard_map.133.refs_11_ = f32[512,1024]{1,0:T(8,128)} custom-call(bf16[3,64,1024]{2,1,0:T(8,128)(2,1)} %shard_map.122.refs_2_.refs_0_.refs_4_, bf16[3,64,1024]{2,1,0:T(8,128)(2,1)} %copy-done.15, bf16[3,192,1024]{2,1,0:T(8,128)(2,1)} %shard_map.132.refs_2_.refs_6_.refs_12_, bf16[3,192,1024]{2,1,0:T(8,128)(2,1)} %copy-done.3, ...), custom_call_target="tpu_custom_call" | custom-call | flops 2147483648 | bytes 4194304 | tf_op jit(solution)/shard_map/pallas_call | solution.py:171
  276.3 12.8 %collective-permute-start.27 = (bf16[128,1024]{1,0:T(8,128)(2,1)S(1)}, bf16[128,1024]{1,0:T(8,128)(2,1)S(1)}, u32[]{:S(2)}, u32[]{:S(2)}) collective-permute-start(bf16[128,1024]{1,0:T(8,128)(2,1)S(1)} %pad_maximum_fusion.2), channel_id=1, source_target_pairs={{0,3},{1,0},{2,1},{3,2},{4,7},{5,4},{6,5},{7,6},{8,11},{9,8},{10,9... | collective-permute-start | bytes 786440 | tf_op jit(solution)/shard_map/ppermute | solution.py:245
  289.9 7.5 %shard_map.134 = (bf16[1024,4096]{1,0:T(8,128)(2,1)}, bf16[1024,4096]{1,0:T(8,128)(2,1)}, bf16[4096,1024]{1,0:T(8,128)(2,1)}, f32[8,128]{1,0:T(8,128)}) custom-call(bf16[3,64,1024]{2,1,0:T(8,128)(2,1)} %shard_map.122.refs_2_.refs_0_.refs_4_, bf16[3,64,1024]{2,1,0:T(8,128)(2,1)} %copy-done.15, ...), custom_call_target="tpu_custom_call", output_to_operand_aliasing={{0}: (8, {}), {1}: (9, {}), {2}: (10, {})} | custom-call | flops 3221225472 | bytes 6291456 | tf_op jit(solution)/shard_map/pallas_call | solution.py:210
  297.4 14.8 %collective-permute-done.28 = bf16[128,1024]{1,0:T(8,128)(2,1)S(1)} collective-permute-done((bf16[128,1024]{1,0:T(8,128)(2,1)S(1)}, bf16[128,1024]{1,0:T(8,128)(2,1)S(1)}, u32[]{:S(2)}, u32[]{:S(2)}) %collective-permute-start.28) | collective-permute-done | bytes 262176 | tf_op jit(solution)/shard_map/ppermute | solution.py:245
  (172 shorter events, 110.7 us)
Async XLA Ops:
  11.5 6.3 %collective-permute-start.1 = (bf16[3,64,1024]{2,1,0:T(8,128)(2,1)}, bf16[3,64,1024]{2,1,0:T(8,128)(2,1)S(1)}, u32[]{:S(2)}, u32[]{:S(2)}) collective-permute-start(bf16[3,64,1024]{2,1,0:T(8,128)(2,1)} %get-tuple-element.35.refs_0_), channel_id=1, source_target_pairs={{0,4},{4,0},{8,12},{12,8},{1,5},{5,1},{9,13},{13,9},{2,6},{6,2},{1... | collective-permute-start | bytes 1179656 | tf_op jit(solution)/shard_map/ppermute | solution.py:263
  17.8 9.0 %collective-permute-start = (bf16[3,64,1024]{2,1,0:T(8,128)(2,1)}, bf16[3,64,1024]{2,1,0:T(8,128)(2,1)S(1)}, u32[]{:S(2)}, u32[]{:S(2)}) collective-permute-start(bf16[3,64,1024]{2,1,0:T(8,128)(2,1)} %get-tuple-element.37.refs_0_), channel_id=1, source_target_pairs={{0,4},{4,0},{8,12},{12,8},{1,5},{5,1},{9,13},{13,9},{2,6},{6,2},{1... | collective-permute-start | bytes 1179656 | tf_op jit(solution)/shard_map/ppermute | solution.py:263
  26.3 16.2 %collective-permute-start.3 = (bf16[3,64,1024]{2,1,0:T(8,128)(2,1)}, bf16[3,64,1024]{2,1,0:T(8,128)(2,1)S(1)}, u32[]{:S(2)}, u32[]{:S(2)}) collective-permute-start(bf16[3,64,1024]{2,1,0:T(8,128)(2,1)} %get-tuple-element.39.refs_0_), channel_id=1, source_target_pairs={{0,4},{4,0},{8,12},{12,8},{1,5},{5,1},{9,13},{13,9},{2,6},{6,2},{1... | collective-permute-start | bytes 1179656 | tf_op jit(solution)/shard_map/ppermute | solution.py:263
  35.3 8.5 %collective-permute-start.2 = (bf16[3,64,1024]{2,1,0:T(8,128)(2,1)}, bf16[3,64,1024]{2,1,0:T(8,128)(2,1)S(1)}, u32[]{:S(2)}, u32[]{:S(2)}) collective-permute-start(bf16[3,64,1024]{2,1,0:T(8,128)(2,1)} %get-tuple-element.41.refs_0_), channel_id=1, source_target_pairs={{0,4},{4,0},{8,12},{12,8},{1,5},{5,1},{9,13},{13,9},{2,6},{6,2},{1... | collective-permute-start | bytes 1179656 | tf_op jit(solution)/shard_map/ppermute | solution.py:263
  35.4 12.8 %collective-permute-start.10 = (bf16[3,64,1024]{2,1,0:T(8,128)(2,1)S(1)}, bf16[3,64,1024]{2,1,0:T(8,128)(2,1)S(1)}, u32[]{:S(2)}, u32[]{:S(2)}) collective-permute-start(bf16[3,64,1024]{2,1,0:T(8,128)(2,1)S(1)} %copy-done.19), channel_id=1, source_target_pairs={{0,8},{4,12},{8,0},{12,4},{1,9},{5,13},{9,1},{13,5},{2,10},{6,14},... | collective-permute-start | bytes 1179656 | tf_op jit(solution)/shard_map/ppermute | solution.py:269
  38.3 30.3 %collective-permute-start.5 = (bf16[2,128,1024]{2,1,0:T(8,128)(2,1)S(1)}, bf16[2,128,1024]{2,1,0:T(8,128)(2,1)S(1)}, u32[]{:S(2)}, u32[]{:S(2)}) collective-permute-start(bf16[2,128,1024]{2,1,0:T(8,128)(2,1)S(1)} %copy-done.2), channel_id=1, source_target_pairs={{0,1},{1,2},{2,3},{3,0},{4,5},{5,6},{6,7},{7,4},{8,9},{9,10},{10,1... | collective-permute-start | bytes 1572872 | tf_op jit(solution)/shard_map/ppermute | solution.py:245
  39.9 36.5 %collective-permute-start.6 = (bf16[2,128,1024]{2,1,0:T(8,128)(2,1)S(1)}, bf16[2,128,1024]{2,1,0:T(8,128)(2,1)S(1)}, u32[]{:S(2)}, u32[]{:S(2)}) collective-permute-start(bf16[2,128,1024]{2,1,0:T(8,128)(2,1)S(1)} %copy-done.2), channel_id=1, source_target_pairs={{0,2},{1,3},{2,0},{3,1},{4,6},{5,7},{6,4},{7,5},{8,10},{9,11},{10,... | collective-permute-start | bytes 1572872 | tf_op jit(solution)/shard_map/ppermute | solution.py:245
  42.5 33.9 %collective-permute-start.7 = (bf16[2,128,1024]{2,1,0:T(8,128)(2,1)S(1)}, bf16[2,128,1024]{2,1,0:T(8,128)(2,1)S(1)}, u32[]{:S(2)}, u32[]{:S(2)}) collective-permute-start(bf16[2,128,1024]{2,1,0:T(8,128)(2,1)S(1)} %copy-done.2), channel_id=1, source_target_pairs={{0,3},{1,0},{2,1},{3,2},{4,7},{5,4},{6,5},{7,6},{8,11},{9,8},{10,9... | collective-permute-start | bytes 1572872 | tf_op jit(solution)/shard_map/ppermute | solution.py:245
  43.8 12.8 %collective-permute-start.9 = (bf16[3,64,1024]{2,1,0:T(8,128)(2,1)S(1)}, bf16[3,64,1024]{2,1,0:T(8,128)(2,1)S(1)}, u32[]{:S(2)}, u32[]{:S(2)}) collective-permute-start(bf16[3,64,1024]{2,1,0:T(8,128)(2,1)S(1)} %copy-done.20), channel_id=1, source_target_pairs={{0,8},{4,12},{8,0},{12,4},{1,9},{5,13},{9,1},{13,5},{2,10},{6,14},... | collective-permute-start | bytes 1179656 | tf_op jit(solution)/shard_map/ppermute | solution.py:269
  48.2 16.3 %collective-permute-start.8 = (bf16[3,64,1024]{2,1,0:T(8,128)(2,1)}, bf16[3,64,1024]{2,1,0:T(8,128)(2,1)S(1)}, u32[]{:S(2)}, u32[]{:S(2)}) collective-permute-start(bf16[3,64,1024]{2,1,0:T(8,128)(2,1)} %shard_map.108.refs_0_), channel_id=1, source_target_pairs={{0,8},{4,12},{8,0},{12,4},{1,9},{5,13},{9,1},{13,5},{2,10},{6,14},... | collective-permute-start | bytes 1179656 | tf_op jit(solution)/shard_map/ppermute | solution.py:269
  87.3 7.8 %collective-permute-start.12 = (bf16[3,192,1024]{2,1,0:T(8,128)(2,1)}, bf16[3,192,1024]{2,1,0:T(8,128)(2,1)S(1)}, u32[]{:S(2)}, u32[]{:S(2)}) collective-permute-start(bf16[3,192,1024]{2,1,0:T(8,128)(2,1)} %get-tuple-element.43.refs_0_), channel_id=1, source_target_pairs={{0,4},{4,0},{8,12},{12,8},{1,5},{5,1},{9,13},{13,9},{2,6},{6,2},{1... | collective-permute-start | bytes 3538952 | tf_op jit(solution)/shard_map/ppermute | solution.py:263
  94.6 11.4 %collective-permute-start.11 = (bf16[3,192,1024]{2,1,0:T(8,128)(2,1)}, bf16[3,192,1024]{2,1,0:T(8,128)(2,1)S(1)}, u32[]{:S(2)}, u32[]{:S(2)}) collective-permute-start(bf16[3,192,1024]{2,1,0:T(8,128)(2,1)} %get-tuple-element.45.refs_0_), channel_id=1, source_target_pairs={{0,4},{4,0},{8,12},{12,8},{1,5},{5,1},{9,13},{13,9},{2,6},{6,2},{1... | collective-permute-start | bytes 3538952 | tf_op jit(solution)/shard_map/ppermute | solution.py:263
  106.0 13.5 %collective-permute-start.14 = (bf16[3,192,1024]{2,1,0:T(8,128)(2,1)}, bf16[3,192,1024]{2,1,0:T(8,128)(2,1)S(1)}, u32[]{:S(2)}, u32[]{:S(2)}) collective-permute-start(bf16[3,192,1024]{2,1,0:T(8,128)(2,1)} %get-tuple-element.47.refs_0_), channel_id=1, source_target_pairs={{0,4},{4,0},{8,12},{12,8},{1,5},{5,1},{9,13},{13,9},{2,6},{6,2},{1... | collective-permute-start | bytes 3538952 | tf_op jit(solution)/shard_map/ppermute | solution.py:263
  117.0 6.1 %collective-permute-start.13 = (bf16[3,192,1024]{2,1,0:T(8,128)(2,1)}, bf16[3,192,1024]{2,1,0:T(8,128)(2,1)S(1)}, u32[]{:S(2)}, u32[]{:S(2)}) collective-permute-start(bf16[3,192,1024]{2,1,0:T(8,128)(2,1)} %get-tuple-element.49.refs_0_), channel_id=1, source_target_pairs={{0,4},{4,0},{8,12},{12,8},{1,5},{5,1},{9,13},{13,9},{2,6},{6,2},{1... | collective-permute-start | bytes 3538952 | tf_op jit(solution)/shard_map/ppermute | solution.py:263
  117.4 40.5 %collective-permute-start.22 = (bf16[3,192,1024]{2,1,0:T(8,128)(2,1)S(1)}, bf16[3,192,1024]{2,1,0:T(8,128)(2,1)S(1)}, u32[]{:S(2)}, u32[]{:S(2)}) collective-permute-start(bf16[3,192,1024]{2,1,0:T(8,128)(2,1)S(1)} %copy-done.7), channel_id=1, source_target_pairs={{0,8},{4,12},{8,0},{12,4},{1,9},{5,13},{9,1},{13,5},{2,10},{6,14},... | collective-permute-start | bytes 3538952 | tf_op jit(solution)/shard_map/ppermute | solution.py:269
  118.0 35.8 %collective-permute-start.4 = (bf16[3,64,1024]{2,1,0:T(8,128)(2,1)S(1)}, bf16[3,64,1024]{2,1,0:T(8,128)(2,1)S(1)}, u32[]{:S(2)}, u32[]{:S(2)}) collective-permute-start(bf16[3,64,1024]{2,1,0:T(8,128)(2,1)S(1)} %copy-done.18), channel_id=1, source_target_pairs={{0,8},{4,12},{8,0},{12,4},{1,9},{5,13},{9,1},{13,5},{2,10},{6,14},... | collective-permute-start | bytes 1179656 | tf_op jit(solution)/shard_map/ppermute | solution.py:269
  163.2 4.5 %collective-permute-start.23 = (bf16[3,192,1024]{2,1,0:T(8,128)(2,1)}, bf16[3,192,1024]{2,1,0:T(8,128)(2,1)S(1)}, u32[]{:S(2)}, u32[]{:S(2)}) collective-permute-start(bf16[3,192,1024]{2,1,0:T(8,128)(2,1)} %shard_map.123.refs_2_.refs_6_.refs_11_), channel_id=1, source_target_pairs={{0,4},{4,0},{8,12},{12,8},{1,5},{5,1},{9,13},{13,9},{2,6},{6,2},{1... | collective-permute-start | bytes 3538952 | tf_op jit(solution)/shard_map/ppermute | solution.py:273
  163.2 28.5 %collective-permute-start.20 = (bf16[3,192,1024]{2,1,0:T(8,128)(2,1)S(1)}, bf16[3,192,1024]{2,1,0:T(8,128)(2,1)}, u32[]{:S(2)}, u32[]{:S(2)}) collective-permute-start(bf16[3,192,1024]{2,1,0:T(8,128)(2,1)S(1)} %copy-done.6), channel_id=1, source_target_pairs={{0,8},{4,12},{8,0},{12,4},{1,9},{5,13},{9,1},{13,5},{2,10},{6,14},... | collective-permute-start | bytes 3538952 | tf_op jit(solution)/shard_map/ppermute | solution.py:269
  163.8 3.9 %collective-permute-start.21 = (bf16[3,64,1024]{2,1,0:T(8,128)(2,1)S(1)}, bf16[3,64,1024]{2,1,0:T(8,128)(2,1)S(1)}, u32[]{:S(2)}, u32[]{:S(2)}) collective-permute-start(bf16[3,64,1024]{2,1,0:T(8,128)(2,1)S(1)} %copy-done.13), channel_id=1, source_target_pairs={{0,4},{4,0},{8,12},{12,8},{1,5},{5,1},{9,13},{13,9},{2,6},{6,2},{1... | collective-permute-start | bytes 1179656 | tf_op jit(solution)/shard_map/ppermute | solution.py:273
  195.8 28.4 %collective-permute-start.18 = (bf16[3,192,1024]{2,1,0:T(8,128)(2,1)S(1)}, bf16[3,192,1024]{2,1,0:T(8,128)(2,1)S(1)}, u32[]{:S(2)}, u32[]{:S(2)}) collective-permute-start(bf16[3,192,1024]{2,1,0:T(8,128)(2,1)S(1)} %copy-done.9), channel_id=1, source_target_pairs={{0,8},{4,12},{8,0},{12,4},{1,9},{5,13},{9,1},{13,5},{2,10},{6,14},... | collective-permute-start | bytes 3538952 | tf_op jit(solution)/shard_map/ppermute | solution.py:269
  229.2 28.4 %collective-permute-start.16 = (bf16[3,192,1024]{2,1,0:T(8,128)(2,1)S(1)}, bf16[3,192,1024]{2,1,0:T(8,128)(2,1)S(1)}, u32[]{:S(2)}, u32[]{:S(2)}) collective-permute-start(bf16[3,192,1024]{2,1,0:T(8,128)(2,1)S(1)} %copy-done.8), channel_id=1, source_target_pairs={{0,8},{4,12},{8,0},{12,4},{1,9},{5,13},{9,1},{13,5},{2,10},{6,14},... | collective-permute-start | bytes 3538952 | tf_op jit(solution)/shard_map/ppermute | solution.py:269
  276.3 21.0 %collective-permute-start.27 = (bf16[128,1024]{1,0:T(8,128)(2,1)S(1)}, bf16[128,1024]{1,0:T(8,128)(2,1)S(1)}, u32[]{:S(2)}, u32[]{:S(2)}) collective-permute-start(bf16[128,1024]{1,0:T(8,128)(2,1)S(1)} %pad_maximum_fusion.2), channel_id=1, source_target_pairs={{0,3},{1,0},{2,1},{3,2},{4,7},{5,4},{6,5},{7,6},{8,11},{9,8},{10,9... | collective-permute-start | bytes 786440 | tf_op jit(solution)/shard_map/ppermute | solution.py:245
  289.2 23.0 %collective-permute-start.28 = (bf16[128,1024]{1,0:T(8,128)(2,1)S(1)}, bf16[128,1024]{1,0:T(8,128)(2,1)S(1)}, u32[]{:S(2)}, u32[]{:S(2)}) collective-permute-start(bf16[128,1024]{1,0:T(8,128)(2,1)S(1)} %pad_maximum_fusion.3), channel_id=1, source_target_pairs={{0,2},{1,3},{2,0},{3,1},{4,6},{5,7},{6,4},{7,5},{8,10},{9,11},{10,... | collective-permute-start | bytes 786440 | tf_op jit(solution)/shard_map/ppermute | solution.py:245
  289.3 22.9 %collective-permute-start.29 = (bf16[128,1024]{1,0:T(8,128)(2,1)S(1)}, bf16[128,1024]{1,0:T(8,128)(2,1)S(1)}, u32[]{:S(2)}, u32[]{:S(2)}) collective-permute-start(bf16[128,1024]{1,0:T(8,128)(2,1)S(1)} %pad_maximum_fusion.4), channel_id=1, source_target_pairs={{0,1},{1,2},{2,3},{3,0},{4,5},{5,6},{6,7},{7,4},{8,9},{9,10},{10,1... | collective-permute-start | bytes 786440 | tf_op jit(solution)/shard_map/ppermute | solution.py:245
  (48 other events, 173.8 us)

commit v4 on v1

v4 whole, which is shorter than its diff:
```python
import functools

import jax
import jax.numpy as jnp
from jax import lax
from jax.experimental import pallas as pl
from jax.experimental.pallas import tpu as pltpu
from jax.sharding import PartitionSpec as P

BLK = 128
STEP = 256
CONTRACT_ROWS = (((0,), (0,)), ((), ()))
CONTRACT_COLUMNS = (((1,), (1,)), ((), ()))
PARAMS = pltpu.CompilerParams(vmem_limit_bytes=40 * 2**20)


def widen(keep, axis):
    return jnp.repeat(keep, BLK, axis=axis).astype(jnp.bfloat16)


def masked(weight, lines):
    rows, columns = weight.shape
    blocked = weight.reshape(rows // BLK, BLK, columns) * lines[:, None, :]
    return blocked.reshape(rows, columns)


def ahead(left, weight):
    return jnp.dot(left, weight, preferred_element_type=jnp.float32)


def behind(left, weight):
    return lax.dot_general(left, weight, CONTRACT_COLUMNS, preferred_element_type=jnp.float32)


def outer(left, right):
    return lax.dot_general(left, right, CONTRACT_ROWS, preferred_element_type=jnp.float32)


def cost(flops, moved):
    return pl.CostEstimate(flops=flops, bytes_accessed=moved, transcendentals=0)


ANY = pl.BlockSpec(memory_space=pl.ANY)


def delta_kernel(n, *refs):
    out_ref = refs[-1]
    gate, up, hidden_delta = (
        functools.reduce(lambda a, b: a + b, [r[i].astype(jnp.float32) for r in refs[:n]]) for i in range(3)
    )
    sigma = jax.nn.sigmoid(gate)
    active = gate * sigma
    out_ref[0] = (active * up).astype(jnp.bfloat16)
    out_ref[1] = (hidden_delta * up * sigma * (1.0 + gate * (1.0 - sigma))).astype(jnp.bfloat16)
    out_ref[2] = (hidden_delta * active).astype(jnp.bfloat16)


def deltas(parts, after):
    three, count, size = parts[0].shape
    step = min(STEP, size)
    spec = pl.BlockSpec((three, count, step), lambda j: (0, 0, j))
    return pl.pallas_call(
        functools.partial(delta_kernel, len(parts)),
        out_shape=jax.ShapeDtypeStruct(parts[0].shape, jnp.bfloat16),
        grid=(size // step,),
        in_specs=[spec] * len(parts) + [ANY] * len(after),
        out_specs=spec,
        compiler_params=PARAMS,
        cost_estimate=cost(60 * count * size, 18 * count * size),
    )(*parts, *after)


def gradient_kernel(n, *refs):
    parts = refs[:n]
    tokens_ref, cotangent_ref, gl_ref, dl_ref = refs[n : n + 4]
    gate_ref, up_ref, down_ref, token_ref = refs[-4:]
    token_ref[...] = jnp.zeros_like(token_ref)

    def put(ref, product, lines):
        rows, columns = product.shape
        blocked = product.reshape(rows // BLK, BLK, columns) * lines.astype(jnp.float32)
        ref[...] = blocked.reshape(rows, columns).astype(jnp.bfloat16)

    hidden, gate_delta, up_delta = (jnp.concatenate([p[i] for p in parts], axis=0) for i in range(3))
    put(gate_ref, ahead(tokens_ref[...], gate_delta), gl_ref[...])
    put(up_ref, ahead(tokens_ref[...], up_delta), gl_ref[...])
    put(down_ref, outer(hidden, cotangent_ref[...]), dl_ref[...])


def gradients(parts, tokens_t, cotangent, lines, k, size, width, into, after):
    height, depth = tokens_t.shape
    step = min(STEP, size)
    base = k * size // step
    n = len(parts)
    columns = pl.BlockSpec((height, step), lambda j: (0, base + j))
    down_rows = pl.BlockSpec((step, height), lambda j: (base + j, 0))
    wide = jax.ShapeDtypeStruct((height, width), jnp.bfloat16)
    return pl.pallas_call(
        functools.partial(gradient_kernel, n),
        out_shape=(wide, wide, jax.ShapeDtypeStruct((width, height), jnp.bfloat16), jax.ShapeDtypeStruct((8, BLK), jnp.float32)),
        grid=(size // step,),
        in_specs=[pl.BlockSpec((3, p.shape[1], step), lambda j: (0, 0, j)) for p in parts]
        + [
            pl.BlockSpec((height, depth), lambda j: (0, 0)),
            pl.BlockSpec((depth, height), lambda j: (0, 0)),
            pl.BlockSpec((height // BLK, 1, step), lambda j: (0, 0, base + j)),
            pl.BlockSpec((step // BLK, 1, height), lambda j: (base + j, 0, 0)),
        ]
        + [ANY] * (len(into) + len(after)),
        out_specs=(columns, columns, down_rows, pl.BlockSpec((8, BLK), lambda j: (0, 0))),
        input_output_aliases={n + 4 + i: i for i in range(len(into))},
        compiler_params=PARAMS,
        cost_estimate=cost(6 * height * depth * size, 6 * height * size),
    )(*parts, tokens_t, cotangent, *lines, *into, *after)


def on_device(n_row, n_col, tokens, cotangent, gate_weight, up_weight, down_weight, gate_keep, down_keep):
    core = lax.rem(lax.axis_index("row"), 2)
    chips = n_row // 2
    swap = [(i, i ^ 1) for i in range(n_row)]
    height, width = gate_weight.shape
    own_rows = tokens.shape[0]
    size = min(1024, width)
    chunks = width // size

    def across(value):
        parts = [value]
        for k in range(1, chips):
            parts.append(lax.ppermute(value, "row", [(i, (i + 2 * k) % n_row) for i in range(n_row)]))
        return parts

    def core_order(value):
        half = value.shape[1] // 2
        mine = lax.dynamic_slice_in_dim(value, core * half, half, 1)
        theirs = lax.dynamic_slice_in_dim(value, (1 - core) * half, half, 1)
        return jnp.concatenate([mine, theirs], axis=1)

    both = jnp.stack([tokens, cotangent])
    blocks = []
    for s in range(1, n_col):
        blocks.append(lax.ppermute(both, "col", [(i, (i + s) % n_col) for i in range(n_col)]))
    own = core_order(both)
    groups = [own]
    if blocks:
        groups.append(jnp.concatenate([core_order(b)[:, : own_rows // 2] for b in blocks] + [core_order(b)[:, own_rows // 2 :] for b in blocks], axis=1))
    rows = jnp.concatenate(groups, axis=1)
    tokens_t = rows[0].T

    gate_lines = widen(gate_keep, 1)
    down_lines = widen(down_keep, 1)

    weights = []
    for k in range(chunks):
        lower = k * size
        lines = gate_lines[:, lower : lower + size]
        weights.append(
            (
                masked(gate_weight[:, lower : lower + size], lines),
                masked(up_weight[:, lower : lower + size], lines),
                masked(down_weight[lower : lower + size], down_lines[lower // BLK : (lower + size) // BLK]),
            )
        )

    def unit(g, k):
        x, (gate, up, down) = groups[g], weights[k]
        half = x.shape[1] // 2
        whole = jnp.stack([ahead(x[0], gate), ahead(x[0], up), behind(x[1], down)]).astype(jnp.bfloat16)
        came = lax.ppermute(whole[:, half:], "row", swap)
        mine = (whole[:, :half].astype(jnp.float32) + came.astype(jnp.float32)).astype(jnp.bfloat16)
        return across(mine)

    def finish(parts, after):
        result = deltas(parts, after)
        return result, lax.ppermute(result, "row", swap)

    order = [(g, k) for g in range(len(groups)) for k in range(chunks)]
    sums = {u: unit(*u) for u in order}
    outs = {(0, k): finish(sums[0, k], []) for k in range(chunks)}
    terms = [0.0] * len(groups)
    line_blocks = (gate_lines[:, None, :], down_lines[:, None, :])
    into, after = (), []
    for k in range(chunks):
        gate, up, down = weights[k]
        for g in range(1, len(groups)):
            outs[g, k] = finish(sums[g, k], after)
        pieces = [p for g in range(len(groups)) for p in outs[g, k]]
        for g in range(len(groups)):
            whole = jnp.concatenate(outs[g, k], axis=1)
            terms[g] = terms[g] + behind(whole[1], gate) + behind(whole[2], up)
        *into, token = gradients(pieces, tokens_t, rows[1], line_blocks, k, size, width, into, [])
        after = [token]

    total = terms[0]
    half = own_rows // 2
    if blocks:
        other = terms[1].astype(jnp.bfloat16)
        middle = half * len(blocks)
        for s in range(1, n_col):
            at = (s - 1) * half
            block = jnp.concatenate([other[at : at + half], other[middle + at : middle + at + half]], axis=0)
            total = total + lax.ppermute(block, "col", [(i, (i - s) % n_col) for i in range(n_col)]).astype(jnp.float32)
    restored = core_order(total[None])[0]
    return (restored.astype(jnp.bfloat16), *into)


def solution(mesh):
    placed = (
        P(("groups", "col"), "row"),
        P(("groups", "col"), "row"),
        P("row", "col"),
        P("row", "col"),
        P("col", "row"),
        P("row", "col"),
        P("col", "row"),
    )
    return jax.shard_map(
        functools.partial(on_device, mesh.shape["row"], mesh.shape["col"]),
        mesh=mesh,
        in_specs=placed,
        out_specs=(
            P(("groups", "col"), "row"),
            P(("groups", "row"), "col"),
            P(("groups", "row"), "col"),
            P(("groups", "col"), "row"),
        ),
        check_vma=False,
    )
```

time: 274 us -> 242 us (0.88)
  waiting for transfers between devices: 93.4 us -> 67.5 us
  matrix products: 37.3 us -> 51.7 us
  other arithmetic: 46.8 us -> 35.2 us
  local copies, waits for them, and re-layouts: 29.6 us -> 24.9 us
    ppermute x16, waiting for transfers between devices: 93.3 us -> 50.2 us  [the longest x8 50.2 us: across(): lax.ppermute(value, 'row', [(i, (i + 2 * k) % n_row) for i in range(n_row)])]
    ppermute x3, waiting for transfers between devices: 0.01 us -> 17.2 us  [on_device(): lax.ppermute(block, 'col', [(i, (i - s) % n_col) for i in range(n_col)])]
    dot_general x24, matrix products: 24.6 us -> 37 us  [behind(): lax.dot_general(left, weight, CONTRACT_COLUMNS, preferred_element_type=jn...]
    add x8 -> x0, other arithmetic: 6.84 us -> none  [across(): total = total + lax.ppermute(value, 'row', pairs).astype(jnp.float32)]
    another operation x16 -> x0, other arithmetic: 3.76 us -> none
    concatenate x4 -> x0, other arithmetic: 2.83 us -> none  [on_device(): h = jnp.concatenate([outs[g, k] for g in range(len(groups))], axis=1)]
    unnamed x105 -> x129, local copies, waits for them, and re-layouts: 17.4 us -> 14.8 us
  transfers between devices with their start and end apart: 30 -> 30, of which waited for: 4 -> 6; matrix products, arithmetic and copies ran while one was open for 35% -> 40% of each run, Pallas kernels for 14% -> 14%
where the time goes in v4:
time: 242 us; the launch traced here: 239 us
  waiting for transfers between devices  67.5 us (28%)
  matrix products  51.7 us (21%)
  other arithmetic  35.2 us (15%)
  Pallas kernels  34.1 us (14%)
  local copies, waits for them, and re-layouts  24.9 us (10%)
  starting transfers between devices  22.9 us (9%)
    ppermute x8, waiting for transfers between devices, across(): lax.ppermute(value, 'row', [(i, (i + 2 * k) % n_row) for i in range(n_row)])  50.2 us
    dot_general x24, matrix products, behind(): lax.dot_general(left, weight, CONTRACT_COLUMNS, preferred_element_type=jn...  37 us
    pallas_call x4, Pallas kernels, gradients(): pl.pallas_call(functools.partial(gradient_kernel, n), out_shape=(wide, wi...  22.8 us
    ppermute x3, waiting for transfers between devices, on_device(): lax.ppermute(block, 'col', [(i, (i - s) % n_col) for i in range(n_col)])  17.2 us
    mul x2, other arithmetic, masked(): blocked = weight.reshape(rows // BLK, BLK, columns) * lines[:, None, :]  15.4 us
    unnamed x129, local copies, waits for them, and re-layouts  14.8 us
    dot_general x16, matrix products, ahead(): return jnp.dot(left, weight, preferred_element_type=jnp.float32)  14.7 us
    pallas_call x8, Pallas kernels, deltas(): pl.pallas_call(functools.partial(delta_kernel, len(parts)), out_shape=jax...  11.3 us
  transfers between devices with their start and end apart: 30, of which 6 were waited for; matrix products, arithmetic and copies ran while one was open for 40% of the time, Pallas kernels for 14%

profile of v4, /device:TPU:0, one launch (start us, length us, event | category | flops | bytes accessed | tf_op | source)
XLA Modules:
  0.0 238.7 jit_solution(3584120736306686484)
XLA Ops:
  0.7 1.9 pad_maximum_fusion.12
  2.6 3.0 %collective-permute-start.12 = (bf16[2,128,1024]{2,1,0:T(8,128)(2,1)}, bf16[2,128,1024]{2,1,0:T(8,128)(2,1)}, u32[]{:S(2)}, u32[]{:S(2)}) collective-permute-start(bf16[2,128,1024]{2,1,0:T(8,128)(2,1)} %pad_maximum_fusion.12), channel_id=1, source_target_pairs={{0,1},{1,2},{2,3},{3,0},{4,5},{5,6},{6,7},{7,4},{8,9},{9,10},{10,1... | collective-permute-start | bytes 1572872 | tf_op jit(solution)/shard_map/ppermute | solution.py:141
  5.6 2.6 %collective-permute-start.13 = (bf16[2,128,1024]{2,1,0:T(8,128)(2,1)}, bf16[2,128,1024]{2,1,0:T(8,128)(2,1)}, u32[]{:S(2)}, u32[]{:S(2)}) collective-permute-start(bf16[2,128,1024]{2,1,0:T(8,128)(2,1)} %pad_maximum_fusion.12), channel_id=1, source_target_pairs={{0,2},{1,3},{2,0},{3,1},{4,6},{5,7},{6,4},{7,5},{8,10},{9,11},{10,... | collective-permute-start | bytes 1572872 | tf_op jit(solution)/shard_map/ppermute | solution.py:141
  12.4 6.7 %bitcast_multiply_fusion.6 = (bf16[1024,1024]{1,0:T(8,128)(2,1)S(1)}, bf16[1024,1024]{1,0:T(8,128)(2,1)S(1)}, bf16[1024,1024]{1,0:T(8,128)(2,1)S(1)}, bf16[1024,...) fusion(bf16[1024,4096]{1,0:T(8,128)(2,1)} %param.10, ...), kind=kLoop, calls=%fused_computation.6 | loop fusion | flops 8388608 | bytes 33619968 | tf_op jit(solution)/shard_map/mul | solution.py:23
  20.2 8.7 %bitcast_multiply_fusion.11 = (bf16[1024,1024]{1,0:T(8,128)(2,1)S(1)}, bf16[1024,1024]{1,0:T(8,128)(2,1)S(1)}, bf16[1024,1024]{1,0:T(8,128)(2,1)S(1)}, bf16[1024,1024]{1,0:T(8,128)(2,1)S(1)}) fusion(bf16[4096,1024]{1,0:T(8,128)(2,1)} %param.11, bf16[8,1024]{1,0:T(8,128)(2,1)S(1)} %get-tuple-element.89, bf16[8,1024]{1,0:T(8,128)(2,1)S(1)} %get-tuple-element.88, ...), kind=kLoop, calls=%fused_computation.19 | loop fusion | flops 4194304 | bytes 16842752 | tf_op jit(solution)/shard_map/mul | solution.py:23
  73.2 1.9 fusion.9
  76.9 1.9 fusion.11
  83.5 16.8 %collective-permute-done.16.refs_1_ = bf16[3,192,1024]{2,1,0:T(8,128)(2,1)S(1)} collective-permute-done((bf16[3,192,1024]{2,1,0:T(8,128)(2,1)S(1)}, bf16[3,192,1024]{2,1,0:T(8,128)(2,1)S(1)}, u32[]{:S(2)}, u32[]{:S(2)}) %collective-permute-start.16) | collective-permute-done | bytes 1179680 | tf_op jit(solution)/shard_map/ppermute | solution.py:129
  114.7 2.3 shard_map.105.refs_0_
  121.4 6.3 %shard_map.107 = (bf16[1024,4096]{1,0:T(8,128)(2,1)}, bf16[1024,4096]{1,0:T(8,128)(2,1)}, bf16[4096,1024]{1,0:T(8,128)(2,1)}, f32[8,128]{1,0:T(8,128)S(1)}) custom-call(bf16[3,64,1024]{2,1,0:T(8,128)(2,1)} %shard_map.102.refs_0_, bf16[3,64,1024]{2,1,0:T(8,128)(2,1)} %collective-permute-done.2.refs_1_, bf16[3,192,1024]{2,1,0:T(8,128)(2,1)S(1)} %shard_map.106.refs_2_, ...), custom_call_target="tpu_custom_call" | custom-call | flops 3221225472 | bytes 6291456 | tf_op jit(solution)/shard_map/pallas_call | solution.py:98
  127.8 5.5 %collective-permute-done.19.refs_1_ = bf16[3,192,1024]{2,1,0:T(8,128)(2,1)} collective-permute-done((bf16[3,192,1024]{2,1,0:T(8,128)(2,1)}, bf16[3,192,1024]{2,1,0:T(8,128)(2,1)}, u32[]{:S(2)}, u32[]{:S(2)}) %collective-permute-start.19) | collective-permute-done | bytes 1179680 | tf_op jit(solution)/shard_map/ppermute | solution.py:129
  133.3 3.0 %shard_map.108.refs_2_ = bf16[3,192,1024]{2,1,0:T(8,128)(2,1)S(1)} custom-call(bf16[3,192,1024]{2,1,0:T(8,128)(2,1)} %add_convert_fusion.2.refs_0_, bf16[3,192,1024]{2,1,0:T(8,128)(2,1)} %collective-permute-done.19.refs_1_, f32[8,128]{1,0:T(8,128)S(1)} %get-tuple-element.19.refs_2_), custom_call_target="tpu_custom_call" | custom-call | flops 11796480 | bytes 3538944 | tf_op jit(solution)/shard_map/pallas_call | solution.py:62
  146.4 5.5 %shard_map.109 = (bf16[1024,4096]{1,0:T(8,128)(2,1)}, bf16[1024,4096]{1,0:T(8,128)(2,1)}, bf16[4096,1024]{1,0:T(8,128)(2,1)}, f32[8,128]{1,0:T(8,128)S(1)}) custom-call(bf16[3,64,1024]{2,1,0:T(8,128)(2,1)S(1)} %shard_map.103.refs_0_, ...), custom_call_target="tpu_custom_call", output_to_operand_aliasing={{0}: (8, {}), {1}: (9, {}), {2}: (10, {})} | custom-call | flops 3221225472 | bytes 6291456 | tf_op jit(solution)/shard_map/pallas_call | solution.py:98
  151.9 14.7 %collective-permute-done.22.refs_1_ = bf16[3,192,1024]{2,1,0:T(8,128)(2,1)S(1)} collective-permute-done((bf16[3,192,1024]{2,1,0:T(8,128)(2,1)S(1)}, bf16[3,192,1024]{2,1,0:T(8,128)(2,1)S(1)}, u32[]{:S(2)}, u32[]{:S(2)}) %collective-permute-start.22) | collective-permute-done | bytes 1179680 | tf_op jit(solution)/shard_map/ppermute | solution.py:129
  167.8 2.2 add_convert_fusion.refs_0_
  173.2 3.3 %fusion.57 = f32[384,1024]{1,0:T(8,128)} fusion(bf16[1024,1024]{1,0:T(8,128)(2,1)S(1)} %copy-done.29, bf16[3,192,1024]{2,1,0:T(8,128)(2,1)} %collective-permute-done.17.refs_3_, bf16[3,192,1024]{2,1,0:T(8,128)(2,1)S(1)} %shard_map.106.refs_2_), kind=kOutput, calls=%fused_computation.107 | convolution fusion | flops 806879232 | bytes 6029312 | tf_op jit(solution)/shard_map/dot_general | solution.py:32
  176.6 3.2 %fusion.60 = f32[384,1024]{1,0:T(8,128)} fusion(bf16[1024,1024]{1,0:T(8,128)(2,1)S(1)} %copy-done.9, bf16[3,192,1024]{2,1,0:T(8,128)(2,1)} %collective-permute-done.17.refs_3_, bf16[3,192,1024]{2,1,0:T(8,128)(2,1)S(1)} %shard_map.106.refs_2_), kind=kOutput, calls=%fused_computation.110 | convolution fusion | flops 806879232 | bytes 6029312 | tf_op jit(solution)/shard_map/dot_general | solution.py:32
  179.8 5.5 %shard_map.111 = (bf16[1024,4096]{1,0:T(8,128)(2,1)}, bf16[1024,4096]{1,0:T(8,128)(2,1)}, bf16[4096,1024]{1,0:T(8,128)(2,1)}, f32[8,128]{1,0:T(8,128)S(1)}) custom-call(bf16[3,64,1024]{2,1,0:T(8,128)(2,1)S(1)} %shard_map.104.refs_0_, ...), custom_call_target="tpu_custom_call", output_to_operand_aliasing={{0}: (8, {}), {1}: (9, {}), {2}: (10, {})} | custom-call | flops 3221225472 | bytes 6291456 | tf_op jit(solution)/shard_map/pallas_call | solution.py:98
  185.2 13.1 %collective-permute-done.25.refs_1_ = bf16[3,192,1024]{2,1,0:T(8,128)(2,1)S(1)} collective-permute-done((bf16[3,192,1024]{2,1,0:T(8,128)(2,1)S(1)}, bf16[3,192,1024]{2,1,0:T(8,128)(2,1)S(1)}, u32[]{:S(2)}, u32[]{:S(2)}) %collective-permute-start.25) | collective-permute-done | bytes 1179680 | tf_op jit(solution)/shard_map/ppermute | solution.py:129
  199.8 2.8 %fusion.53 = f32[384,1024]{1,0:T(8,128)S(1)} fusion(bf16[1024,1024]{1,0:T(8,128)(2,1)} %copy-done.23, bf16[3,192,1024]{2,1,0:T(8,128)(2,1)S(1)} %collective-permute-done.20.refs_3_, bf16[3,192,1024]{2,1,0:T(8,128)(2,1)S(1)} %shard_map.108.refs_2_), kind=kOutput, calls=%fused_computation.102 | convolution fusion | flops 806879232 | bytes 6029312 | tf_op jit(solution)/shard_map/dot_general | solution.py:32
  209.9 2.1 collective-permute-start.27
  212.7 5.5 %shard_map.113 = (bf16[1024,4096]{1,0:T(8,128)(2,1)}, bf16[1024,4096]{1,0:T(8,128)(2,1)}, bf16[4096,1024]{1,0:T(8,128)(2,1)}, f32[8,128]{1,0:T(8,128)}) custom-call(bf16[3,64,1024]{2,1,0:T(8,128)(2,1)S(1)} %shard_map.105.refs_0_, ...), custom_call_target="tpu_custom_call", output_to_operand_aliasing={{0}: (8, {}), {1}: (9, {}), {2}: (10, {})} | custom-call | flops 3221225472 | bytes 6291456 | tf_op jit(solution)/shard_map/pallas_call | solution.py:98
  218.7 16.8 %collective-permute-done.28 = bf16[128,1024]{1,0:T(8,128)(2,1)S(1)} collective-permute-done((bf16[128,1024]{1,0:T(8,128)(2,1)S(1)}, bf16[128,1024]{1,0:T(8,128)(2,1)S(1)}, u32[]{:S(2)}, u32[]{:S(2)}) %collective-permute-start.28) | collective-permute-done | bytes 262176 | tf_op jit(solution)/shard_map/ppermute | solution.py:201
  235.6 2.0 fusion.20
  (267 shorter events, 98.8 us)
Async XLA Ops:
  2.6 46.8 %collective-permute-start.12 = (bf16[2,128,1024]{2,1,0:T(8,128)(2,1)}, bf16[2,128,1024]{2,1,0:T(8,128)(2,1)}, u32[]{:S(2)}, u32[]{:S(2)}) collective-permute-start(bf16[2,128,1024]{2,1,0:T(8,128)(2,1)} %pad_maximum_fusion.12), channel_id=1, source_target_pairs={{0,1},{1,2},{2,3},{3,0},{4,5},{5,6},{6,7},{7,4},{8,9},{9,10},{10,1... | collective-permute-start | bytes 1572872 | tf_op jit(solution)/shard_map/ppermute | solution.py:141
  5.6 46.3 %collective-permute-start.13 = (bf16[2,128,1024]{2,1,0:T(8,128)(2,1)}, bf16[2,128,1024]{2,1,0:T(8,128)(2,1)}, u32[]{:S(2)}, u32[]{:S(2)}) collective-permute-start(bf16[2,128,1024]{2,1,0:T(8,128)(2,1)} %pad_maximum_fusion.12), channel_id=1, source_target_pairs={{0,2},{1,3},{2,0},{3,1},{4,6},{5,7},{6,4},{7,5},{8,10},{9,11},{10,... | collective-permute-start | bytes 1572872 | tf_op jit(solution)/shard_map/ppermute | solution.py:141
  8.2 44.7 %collective-permute-start.14 = (bf16[2,128,1024]{2,1,0:T(8,128)(2,1)}, bf16[2,128,1024]{2,1,0:T(8,128)(2,1)}, u32[]{:S(2)}, u32[]{:S(2)}) collective-permute-start(bf16[2,128,1024]{2,1,0:T(8,128)(2,1)} %pad_maximum_fusion.12), channel_id=1, source_target_pairs={{0,3},{1,0},{2,1},{3,2},{4,7},{5,4},{6,5},{7,6},{8,11},{9,8},{10,9... | collective-permute-start | bytes 1572872 | tf_op jit(solution)/shard_map/ppermute | solution.py:141
  31.3 11.9 %collective-permute-start = (bf16[3,64,1024]{2,1,0:T(8,128)(2,1)}, bf16[3,64,1024]{2,1,0:T(8,128)(2,1)}, u32[]{:S(2)}, u32[]{:S(2)}) collective-permute-start(bf16[3,64,1024]{2,1,0:T(8,128)(2,1)} %slice.303), channel_id=1, source_target_pairs={{0,4},{4,0},{8,12},{12,8},{1,5},{5,1},{9,13},{13,9},{2,6},{6,2},{1... | collective-permute-start | bytes 1179656 | tf_op jit(solution)/shard_map/ppermute | solution.py:168
  34.0 10.5 %collective-permute-start.3 = (bf16[3,64,1024]{2,1,0:T(8,128)(2,1)}, bf16[3,64,1024]{2,1,0:T(8,128)(2,1)}, u32[]{:S(2)}, u32[]{:S(2)}) collective-permute-start(bf16[3,64,1024]{2,1,0:T(8,128)(2,1)} %slice.306), channel_id=1, source_target_pairs={{0,4},{4,0},{8,12},{12,8},{1,5},{5,1},{9,13},{13,9},{2,6},{6,2},{1... | collective-permute-start | bytes 1179656 | tf_op jit(solution)/shard_map/ppermute | solution.py:168
  46.2 34.2 %collective-permute-start.1 = (bf16[3,64,1024]{2,1,0:T(8,128)(2,1)S(1)}, bf16[3,64,1024]{2,1,0:T(8,128)(2,1)S(1)}, u32[]{:S(2)}, u32[]{:S(2)}) collective-permute-start(bf16[3,64,1024]{2,1,0:T(8,128)(2,1)S(1)} %add_convert_fusion.8.refs_0_), channel_id=1, source_target_pairs={{0,8},{4,12},{8,0},{12,4},{1,9},{5,13},{9,1},{13,5},{2,10},{6,14},... | collective-permute-start | bytes 1179656 | tf_op jit(solution)/shard_map/ppermute | solution.py:129
  47.9 55.7 %collective-permute-start.4 = (bf16[3,64,1024]{2,1,0:T(8,128)(2,1)S(1)}, bf16[3,64,1024]{2,1,0:T(8,128)(2,1)S(1)}, u32[]{:S(2)}, u32[]{:S(2)}) collective-permute-start(bf16[3,64,1024]{2,1,0:T(8,128)(2,1)S(1)} %add_convert_fusion.7.refs_0_), channel_id=1, source_target_pairs={{0,8},{4,12},{8,0},{12,4},{1,9},{5,13},{9,1},{13,5},{2,10},{6,14},... | collective-permute-start | bytes 1179656 | tf_op jit(solution)/shard_map/ppermute | solution.py:129
  49.4 54.2 %collective-permute-start.7 = (bf16[3,64,1024]{2,1,0:T(8,128)(2,1)S(1)}, bf16[3,64,1024]{2,1,0:T(8,128)(2,1)S(1)}, u32[]{:S(2)}, u32[]{:S(2)}) collective-permute-start(bf16[3,64,1024]{2,1,0:T(8,128)(2,1)S(1)} %add_convert_fusion.6.refs_0_), channel_id=1, source_target_pairs={{0,8},{4,12},{8,0},{12,4},{1,9},{5,13},{9,1},{13,5},{2,10},{6,14},... | collective-permute-start | bytes 1179656 | tf_op jit(solution)/shard_map/ppermute | solution.py:129
  67.2 34.3 %collective-permute-start.18 = (bf16[3,192,1024]{2,1,0:T(8,128)(2,1)S(1)}, bf16[3,192,1024]{2,1,0:T(8,128)(2,1)S(1)}, u32[]{:S(2)}, u32[]{:S(2)}) collective-permute-start(bf16[3,192,1024]{2,1,0:T(8,128)(2,1)S(1)} %slice.318), channel_id=1, source_target_pairs={{0,4},{4,0},{8,12},{12,8},{1,5},{5,1},{9,13},{13,9},{2,6},{6,2},{1... | collective-permute-start | bytes 3538952 | tf_op jit(solution)/shard_map/ppermute | solution.py:168
  71.0 29.3 %collective-permute-start.16 = (bf16[3,192,1024]{2,1,0:T(8,128)(2,1)S(1)}, bf16[3,192,1024]{2,1,0:T(8,128)(2,1)S(1)}, u32[]{:S(2)}, u32[]{:S(2)}) collective-permute-start(bf16[3,192,1024]{2,1,0:T(8,128)(2,1)S(1)} %add_convert_fusion.3.refs_0_), channel_id=1, source_target_pairs={{0,8},{4,12},{8,0},{12,4},{1,9},{5,13},{9,1},{13,5},{2,10},{6,14},... | collective-permute-start | bytes 3538952 | tf_op jit(solution)/shard_map/ppermute | solution.py:129
  80.9 29.4 %collective-permute-start.10 = (bf16[3,64,1024]{2,1,0:T(8,128)(2,1)}, bf16[3,64,1024]{2,1,0:T(8,128)(2,1)}, u32[]{:S(2)}, u32[]{:S(2)}) collective-permute-start(bf16[3,64,1024]{2,1,0:T(8,128)(2,1)} %add_convert_fusion.5.refs_0_), channel_id=1, source_target_pairs={{0,8},{4,12},{8,0},{12,4},{1,9},{5,13},{9,1},{13,5},{2,10},{6,14},... | collective-permute-start | bytes 1179656 | tf_op jit(solution)/shard_map/ppermute | solution.py:129
  100.4 36.0 %collective-permute-start.21 = (bf16[3,192,1024]{2,1,0:T(8,128)(2,1)}, bf16[3,192,1024]{2,1,0:T(8,128)(2,1)}, u32[]{:S(2)}, u32[]{:S(2)}) collective-permute-start(bf16[3,192,1024]{2,1,0:T(8,128)(2,1)} %slice.322), channel_id=1, source_target_pairs={{0,4},{4,0},{8,12},{12,8},{1,5},{5,1},{9,13},{13,9},{2,6},{6,2},{1... | collective-permute-start | bytes 3538952 | tf_op jit(solution)/shard_map/ppermute | solution.py:168
  101.5 19.6 %collective-permute-start.17 = (bf16[3,192,1024]{2,1,0:T(8,128)(2,1)S(1)}, bf16[3,192,1024]{2,1,0:T(8,128)(2,1)}, u32[]{:S(2)}, u32[]{:S(2)}) collective-permute-start(bf16[3,192,1024]{2,1,0:T(8,128)(2,1)S(1)} %shard_map.106.refs_2_), channel_id=1, source_target_pairs={{0,4},{4,0},{8,12},{12,8},{1,5},{5,1},{9,13},{13,9},{2,6},{6,2},{1... | collective-permute-start | bytes 3538952 | tf_op jit(solution)/shard_map/ppermute | solution.py:174
  103.6 13.3 %collective-permute-start.2 = (bf16[3,64,1024]{2,1,0:T(8,128)(2,1)}, bf16[3,64,1024]{2,1,0:T(8,128)(2,1)}, u32[]{:S(2)}, u32[]{:S(2)}) collective-permute-start(bf16[3,64,1024]{2,1,0:T(8,128)(2,1)} %shard_map.102.refs_0_), channel_id=1, source_target_pairs={{0,4},{4,0},{8,12},{12,8},{1,5},{5,1},{9,13},{13,9},{2,6},{6,2},{1... | collective-permute-start | bytes 1179656 | tf_op jit(solution)/shard_map/ppermute | solution.py:174
  103.7 29.7 %collective-permute-start.19 = (bf16[3,192,1024]{2,1,0:T(8,128)(2,1)}, bf16[3,192,1024]{2,1,0:T(8,128)(2,1)}, u32[]{:S(2)}, u32[]{:S(2)}) collective-permute-start(bf16[3,192,1024]{2,1,0:T(8,128)(2,1)} %add_convert_fusion.2.refs_0_), channel_id=1, source_target_pairs={{0,8},{4,12},{8,0},{12,4},{1,9},{5,13},{9,1},{13,5},{2,10},{6,14},... | collective-permute-start | bytes 3538952 | tf_op jit(solution)/shard_map/ppermute | solution.py:129
  117.0 50.8 %collective-permute-start.24 = (bf16[3,192,1024]{2,1,0:T(8,128)(2,1)}, bf16[3,192,1024]{2,1,0:T(8,128)(2,1)}, u32[]{:S(2)}, u32[]{:S(2)}) collective-permute-start(bf16[3,192,1024]{2,1,0:T(8,128)(2,1)} %slice.324), channel_id=1, source_target_pairs={{0,4},{4,0},{8,12},{12,8},{1,5},{5,1},{9,13},{13,9},{2,6},{6,2},{1... | collective-permute-start | bytes 3538952 | tf_op jit(solution)/shard_map/ppermute | solution.py:168
  119.2 22.3 %collective-permute-start.8 = (bf16[3,64,1024]{2,1,0:T(8,128)(2,1)S(1)}, bf16[3,64,1024]{2,1,0:T(8,128)(2,1)S(1)}, u32[]{:S(2)}, u32[]{:S(2)}) collective-permute-start(bf16[3,64,1024]{2,1,0:T(8,128)(2,1)S(1)} %shard_map.104.refs_0_), channel_id=1, source_target_pairs={{0,4},{4,0},{8,12},{12,8},{1,5},{5,1},{9,13},{13,9},{2,6},{6,2},{1... | collective-permute-start | bytes 1179656 | tf_op jit(solution)/shard_map/ppermute | solution.py:174
  121.1 23.6 %collective-permute-start.11 = (bf16[3,64,1024]{2,1,0:T(8,128)(2,1)S(1)}, bf16[3,64,1024]{2,1,0:T(8,128)(2,1)S(1)}, u32[]{:S(2)}, u32[]{:S(2)}) collective-permute-start(bf16[3,64,1024]{2,1,0:T(8,128)(2,1)S(1)} %shard_map.105.refs_0_), channel_id=1, source_target_pairs={{0,4},{4,0},{8,12},{12,8},{1,5},{5,1},{9,13},{13,9},{2,6},{6,2},{1... | collective-permute-start | bytes 1179656 | tf_op jit(solution)/shard_map/ppermute | solution.py:174
  136.3 10.1 %collective-permute-start.20 = (bf16[3,192,1024]{2,1,0:T(8,128)(2,1)S(1)}, bf16[3,192,1024]{2,1,0:T(8,128)(2,1)S(1)}, u32[]{:S(2)}, u32[]{:S(2)}) collective-permute-start(bf16[3,192,1024]{2,1,0:T(8,128)(2,1)S(1)} %shard_map.108.refs_2_), channel_id=1, source_target_pairs={{0,4},{4,0},{8,12},{12,8},{1,5},{5,1},{9,13},{13,9},{2,6},{6,2},{1... | collective-permute-start | bytes 3538952 | tf_op jit(solution)/shard_map/ppermute | solution.py:174
  138.3 28.3 %collective-permute-start.22 = (bf16[3,192,1024]{2,1,0:T(8,128)(2,1)S(1)}, bf16[3,192,1024]{2,1,0:T(8,128)(2,1)S(1)}, u32[]{:S(2)}, u32[]{:S(2)}) collective-permute-start(bf16[3,192,1024]{2,1,0:T(8,128)(2,1)S(1)} %add_convert_fusion.1.refs_0_), channel_id=1, source_target_pairs={{0,8},{4,12},{8,0},{12,4},{1,9},{5,13},{9,1},{13,5},{2,10},{6,14},... | collective-permute-start | bytes 3538952 | tf_op jit(solution)/shard_map/ppermute | solution.py:129
  167.7 12.1 %collective-permute-start.23 = (bf16[3,192,1024]{2,1,0:T(8,128)(2,1)S(1)}, bf16[3,192,1024]{2,1,0:T(8,128)(2,1)S(1)}, u32[]{:S(2)}, u32[]{:S(2)}) collective-permute-start(bf16[3,192,1024]{2,1,0:T(8,128)(2,1)S(1)} %shard_map.110.refs_2_), channel_id=1, source_target_pairs={{0,4},{4,0},{8,12},{12,8},{1,5},{5,1},{9,13},{13,9},{2,6},{6,2},{1... | collective-permute-start | bytes 3538952 | tf_op jit(solution)/shard_map/ppermute | solution.py:174
  170.0 28.3 %collective-permute-start.25 = (bf16[3,192,1024]{2,1,0:T(8,128)(2,1)S(1)}, bf16[3,192,1024]{2,1,0:T(8,128)(2,1)S(1)}, u32[]{:S(2)}, u32[]{:S(2)}) collective-permute-start(bf16[3,192,1024]{2,1,0:T(8,128)(2,1)S(1)} %add_convert_fusion.refs_0_), channel_id=1, source_target_pairs={{0,8},{4,12},{8,0},{12,4},{1,9},{5,13},{9,1},{13,5},{2,10},{6,14},... | collective-permute-start | bytes 3538952 | tf_op jit(solution)/shard_map/ppermute | solution.py:129
  212.0 23.5 %collective-permute-start.28 = (bf16[128,1024]{1,0:T(8,128)(2,1)S(1)}, bf16[128,1024]{1,0:T(8,128)(2,1)S(1)}, u32[]{:S(2)}, u32[]{:S(2)}) collective-permute-start(bf16[128,1024]{1,0:T(8,128)(2,1)S(1)} %pad_maximum_fusion.19), channel_id=1, source_target_pairs={{0,2},{1,3},{2,0},{3,1},{4,6},{5,7},{6,4},{7,5},{8,10},{9,11},{10,... | collective-permute-start | bytes 786440 | tf_op jit(solution)/shard_map/ppermute | solution.py:201
  212.3 23.3 %collective-permute-start.29 = (bf16[128,1024]{1,0:T(8,128)(2,1)S(1)}, bf16[128,1024]{1,0:T(8,128)(2,1)S(1)}, u32[]{:S(2)}, u32[]{:S(2)}) collective-permute-start(bf16[128,1024]{1,0:T(8,128)(2,1)S(1)} %pad_maximum_fusion.20), channel_id=1, source_target_pairs={{0,1},{1,2},{2,3},{3,0},{4,5},{5,6},{6,7},{7,4},{8,9},{9,10},{10,1... | collective-permute-start | bytes 786440 | tf_op jit(solution)/shard_map/ppermute | solution.py:201
  (67 other events, 501.6 us)
